TPU v7x, 32 devices: a whole 2x2x4 slice. The times are simulated.
32 devices in a mesh: seq: 16 (over z, y, x), tp: 2 (over core).
Axes of the slice: x: 2, y: 2, z: 4, core: 2. Of those that a mesh axis runs over, the one named last changes fastest.
Arguments:
- tokens: bfloat16 [4096, 4096], P('seq', 'tp'), may hold values from -6 to 6
- x_weight: bfloat16 [4096, 2048], P('seq', 'tp'), may hold values from -0.09375 to 0.09375
- bc_weight: bfloat16 [4096, 256], P('seq', 'tp'), may hold values from -0.09375 to 0.09375
- dt_weight: bfloat16 [4096, 32], P('seq', 'tp'), may hold values from -0.09375 to 0.09375
- conv_x: float32 [4, 2048], P(None, 'tp'), may hold values from -2.5 to 2.5
- conv_bc: float32 [4, 256], replicated, may hold values from -2.5 to 2.5
- dt_bias: float32 [32], P('tp'), may hold values from -3 to 0
- decay_rate: float32 [32], P('tp'), may hold values from 2.4414062e-06 to 0.07
- d_skip: float32 [32], P('tp'), may hold values from 0.5 to 2
- norm_gain: float32 [2048], P('tp'), may hold values from 0.5 to 1.5
- initial_state: float32 [32, 64, 128], P('tp'), may hold values from -16 to 16
- steer: float32 [2048], P('tp'), may hold values from -6 to 6
Outputs:
- steered: bfloat16 [4096, 2048], P('seq', 'tp')
All inputs are finite; a program needn't handle non-finite values.
Results may differ from a plain program's by a relative error of at most 0.0055.
Values may be sent and summed in bfloat16 or wider, within the bound.
A program may use at most 64 MiB of HBM per device.

v0:
```python
import jax
import jax.numpy as jnp
from jax import lax
from jax.sharding import PartitionSpec as P

N = 128
GROUP = 128


EPSILON = 1e-05


def passed_along(value, axis, steps):
    count = lax.axis_size(axis)
    first, last = (max(0, -steps), min(count, count - steps))
    return lax.ppermute(value, axis, [(source, source + steps) for source in range(first, last)])


def prefix(x, axis, combine, identity):
    count, mine = (lax.axis_size(axis), lax.axis_index(axis))
    everything = jax.tree.map(
        lambda part, kind: lax.all_gather(part.astype(kind), axis), x, (jnp.bfloat16, jnp.bfloat16)
    )
    start = jax.tree.map(
        lambda part, zero: jnp.broadcast_to(jnp.asarray(zero, part.dtype), part.shape), x, identity
    )

    def turn(k, before):
        reached = k < mine
        new = combine(
            before, jax.tree.map(lambda part, own: part[k].astype(own.dtype), everything, x)
        )
        return jax.tree.map(lambda a, b: jnp.where(reached, a, b), new, before)

    return lax.fori_loop(0, count, turn, start)


def convolve(extended, kernel):
    kernel_rows = kernel.shape[0]
    length = extended.shape[0] - kernel_rows + 1
    summed = kernel[0] * extended[0:length].astype(jnp.float32)
    for offset in range(1, kernel_rows):
        summed = summed + kernel[offset] * extended[offset : offset + length].astype(jnp.float32)
    return jax.nn.silu(summed).astype(jnp.bfloat16)


def block_update(carry_state, inputs):
    x_block, b_block, c_block, a_block, dt_block = inputs
    length = a_block.shape[0]
    cumulative = jnp.cumsum(a_block, axis=0)
    scores = jnp.dot(c_block, b_block.T, preferred_element_type=jnp.float32)
    causal = lax.broadcasted_iota(jnp.int32, (length, length), 0) >= lax.broadcasted_iota(
        jnp.int32, (length, length), 1
    )
    differ = cumulative[:, None, :] - cumulative[None, :, :]
    decays = jnp.where(causal[:, :, None], jnp.exp(jnp.where(causal[:, :, None], differ, 0.0)), 0.0)
    mixing = (scores[:, :, None] * decays * dt_block[None, :, :]).astype(jnp.bfloat16)
    inside = jnp.einsum("tsh,shp->thp", mixing, x_block, preferred_element_type=jnp.float32)
    carried_in = jnp.einsum(
        "tn,hpn->thp", c_block.astype(jnp.float32), carry_state, precision=lax.Precision.HIGHEST
    )
    outputs = inside + jnp.exp(cumulative)[:, :, None] * carried_in
    to_end = jnp.exp(cumulative[-1][None, :] - cumulative) * dt_block
    scaled = (x_block.astype(jnp.float32) * to_end[:, :, None]).astype(jnp.bfloat16)
    added_state = jnp.einsum("shp,sn->hpn", scaled, b_block, preferred_element_type=jnp.float32)
    return (jnp.exp(cumulative[-1])[:, None, None] * carry_state + added_state, outputs)


def combine_carry(earlier, later):
    return (earlier[0] * later[0], later[0][:, None, None] * earlier[1] + later[1])


def per_device(
    tokens,
    x_weight,
    bc_weight,
    dt_weight,
    conv_x,
    conv_bc,
    dt_bias,
    decay_rate,
    d_skip,
    norm_gain,
    initial_state,
    steer,
):
    features = lax.all_gather(tokens, "tp", axis=1, tiled=True)
    rim_rows = conv_x.shape[0] - 1
    local_tokens = features.shape[0]
    head_count = dt_weight.shape[1]
    channels = x_weight.shape[1]
    head_size = channels // head_count
    bc_panel = lax.all_gather(bc_weight, "tp", axis=1, tiled=True)
    previous = passed_along(features[local_tokens - rim_rows :], "seq", 1)
    source = jnp.concatenate([previous, features], 0)
    x_sums = jnp.dot(
        source,
        lax.all_gather(x_weight, "seq", axis=0, tiled=True),
        preferred_element_type=jnp.float32,
    )
    bc_sums = jnp.dot(
        source,
        lax.all_gather(bc_panel, "seq", axis=0, tiled=True),
        preferred_element_type=jnp.float32,
    )
    dt_sums = jnp.dot(
        source,
        lax.all_gather(dt_weight, "seq", axis=0, tiled=True),
        preferred_element_type=jnp.float32,
    )
    x_pre = x_sums.astype(jnp.bfloat16)
    bc_pre = bc_sums.astype(jnp.bfloat16)
    dt_raw = dt_sums[rim_rows:]
    x_conv = convolve(x_pre, conv_x)
    bc_conv = convolve(bc_pre, conv_bc)
    b_values = bc_conv[:, :N]
    c_values = bc_conv[:, N:]
    step_size = jax.nn.softplus(dt_raw + dt_bias[None, :])
    log_decay = -step_size * decay_rate[None, :]
    blocks = local_tokens // GROUP
    x_heads = x_conv.reshape(local_tokens, head_count, head_size)
    inputs = (
        x_heads.reshape(blocks, GROUP, head_count, head_size),
        b_values.reshape(blocks, GROUP, N),
        c_values.reshape(blocks, GROUP, N),
        log_decay.reshape(blocks, GROUP, head_count),
        step_size.reshape(blocks, GROUP, head_count),
    )
    zero_state = jnp.zeros((head_count, head_size, N), jnp.float32)
    local_state, local_out = lax.scan(block_update, zero_state, inputs)
    running = jnp.cumsum(log_decay, axis=0)
    local_decay = jnp.exp(running[-1])
    identity = (
        jnp.ones((head_count,), jnp.float32),
        jnp.zeros((head_count, head_size, N), jnp.float32),
    )
    prefix_decay, prefix_state = prefix((local_decay, local_state), "seq", combine_carry, identity)
    entering = prefix_decay[:, None, None] * initial_state + prefix_state
    from_entering = jnp.einsum(
        "tn,hpn->thp", c_values.astype(jnp.float32), entering, precision=lax.Precision.HIGHEST
    )
    outputs = (
        local_out.reshape(local_tokens, head_count, head_size)
        + jnp.exp(running)[:, :, None] * from_entering
        + d_skip[None, :, None] * x_heads.astype(jnp.float32)
    )
    mean_square = jnp.mean(outputs * outputs, axis=-1, keepdims=True)
    normed = (outputs * lax.rsqrt(mean_square + EPSILON)).reshape(
        local_tokens, channels
    ) * norm_gain[None, :]
    partial_dot = jnp.sum(normed * steer[None, :], axis=1)
    total_dot = lax.psum(partial_dot, "tp")
    penalty = total_dot / jnp.sqrt(jnp.float32(channels * lax.axis_size("tp")))
    return (normed - penalty[:, None] * steer[None, :]).astype(jnp.bfloat16)


def solution(mesh):
    placed = (
        P("seq", "tp"),
        P("seq", "tp"),
        P("seq", "tp"),
        P("seq", "tp"),
        P(None, "tp"),
        P(),
        P("tp"),
        P("tp"),
        P("tp"),
        P("tp"),
        P("tp", None, None),
        P("tp"),
    )
    return jax.shard_map(
        per_device, mesh=mesh, in_specs=placed, out_specs=P("seq", "tp"), check_vma=False
    )
```

profile of v0, /device:TPU:0, one launch (start us, length us, event | category | flops | bytes accessed | tf_op | source)
XLA Modules:
  0.0 344.9 jit_solution(14921733249764642283)
XLA Ops:
  7.3 3.7 %all_gather.28 = bf16[256,256]{1,0:T(8,128)(2,1)} all-gather(bf16[256,128]{1,0:T(8,128)(2,1)} %param.18), channel_id=1, replica_groups=mesh['seq'=16,'tp'=2] {'tp'}, dimensions={1}, use_global_device_ids=true | all-gather | bytes 196608 | tf_op jit(solution)/shard_map/all_gather | solution.py:93
  13.5 8.7 %all-gather.7.cloned.1.call-done = bf16[256,4096]{1,0:T(8,128)(2,1)} async-done(((bf16[256,2048]{1,0:T(8,128)(2,1)}), bf16[256,4096]{1,0:T(8,128)(2,1)}) %all-gather.7.cloned.1.call-update) | async-done | bytes 2097168 | tf_op jit(solution)/shard_map/all_gather | solution.py:87
  23.1 3.6 %collective-permute-start = (bf16[3,4096]{1,0:T(4,128)(2,1)S(1)}, bf16[3,4096]{1,0:T(4,128)(2,1)S(1)}, u32[]{:S(2)}, u32[]{:S(2)}) collective-permute-start(bf16[3,4096]{1,0:T(4,128)(2,1)S(1)} %slice.99), channel_id=1, source_target_pairs={{0,2},{2,4},{4,6},{6,8},{8,10},{10,12},{12,14},{14,16},{16,18},{18... | collective-permute-start | bytes 73736 | tf_op jit(solution)/shard_map/ppermute | solution.py:16
  26.7 39.7 %all_gather.26 = bf16[4096,16]{0,1:T(8,128)(2,1)S(1)} all-gather(bf16[256,16]{0,1:T(8,128)(2,1)} %param.19), channel_id=1, replica_groups=mesh['seq'=16,'tp'=2] {'seq'}, dimensions={0}, use_global_device_ids=true | all-gather | bytes 139264 | tf_op jit(solution)/shard_map/all_gather | solution.py:108
  66.4 2.3 negate_multiply_fusion
  68.9 18.1 %all-gather.11.cloned.1.call-done = bf16[4096,256]{1,0:T(8,128)(2,1)} async-done(((bf16[256,256]{1,0:T(8,128)(2,1)}), bf16[4096,256]{1,0:T(8,128)(2,1)}) %all-gather.11.cloned.1.call-update) | async-done | bytes 2097168 | tf_op jit(solution)/shard_map/all_gather | solution.py:103
  87.0 3.0 fusion.42
  90.2 111.2 %all-gather.9.cloned.1.call-done = bf16[4096,1024]{1,0:T(8,128)(2,1)} async-done(((bf16[256,1024]{1,0:T(8,128)(2,1)}), bf16[4096,1024]{1,0:T(8,128)(2,1)}) %all-gather.9.cloned.1.call-update) | async-done | bytes 8388624 | tf_op jit(solution)/shard_map/all_gather | solution.py:98
  201.4 6.4 %fusion.41 = bf16[259,1024]{1,0:T(8,128)(2,1)S(1)} fusion(bf16[4096,1024]{1,0:T(8,128)(2,1)} %all-gather.9.cloned.1.call-done, bf16[256,4096]{1,0:T(8,128)(2,1)} %all-gather.7.cloned.1.call-done, bf16[3,4096]{1,0:T(4,128)(2,1)S(1)} %collective-permute-done), kind=kOutput, calls=%fused_computation.56 | convolution fusion | flops 2177158144 | bytes 11040768 | tf_op jit(solution)/shard_map/dot_general | solution.py:96
  210.1 29.9 %while.29 = (s32[]{:T(128)}, f32[16,64,128]{2,1,0:T(8,128)S(1)}, f32[2,128,16,64]{1,0,3,2:T(2,128)}, f32[2,128,16]{2,1,0:T(8,128)S(1)}, bf16[2,128,16,64]{1,3,2,...) while((s32[]{:T(128)}, f32[16,64,128]{2,1,0:T(8,128)S(1)}, ...), condition=%wide.region_2.3_spmd.clone, body=%wide.region_0.2_spmd.clone.sunk | while | flops 275662848 | bytes 5197271 | solution.py:130
  212.0 13.1 %dynamic_update_slice.6 = f32[2,128,16,64]{1,0,3,2:T(2,128)} dynamic-update-slice(f32[2,128,16,64]{1,0,3,2:T(2,128)} %get-tuple-element.400, f32[1,128,16,64]{1,0,3,2:T(1,128)S(1)} %bitcast.110, s32[]{:T(128)S(6)} %copy.99, s32[]{:T(128)} %constant.65.clone.1..sunk, s32[]{:T(128)} %constant.65.clone.1..sunk, s32[]{:T(128)} %constant.65.clone.1..sunk) | dynamic-update-slice | bytes 1048580 | tf_op jit(solution)/shard_map/while/body/jit(dynamic_update_index_in_dim)/dynamic_update_slice | solution.py:130
  226.9 13.1 %dynamic_update_slice.6 = f32[2,128,16,64]{1,0,3,2:T(2,128)} dynamic-update-slice(f32[2,128,16,64]{1,0,3,2:T(2,128)} %get-tuple-element.400, f32[1,128,16,64]{1,0,3,2:T(1,128)S(1)} %bitcast.110, s32[]{:T(128)S(6)} %copy.99, s32[]{:T(128)} %constant.65.clone.1..sunk, s32[]{:T(128)} %constant.65.clone.1..sunk, s32[]{:T(128)} %constant.65.clone.1..sunk) | dynamic-update-slice | bytes 1048580 | tf_op jit(solution)/shard_map/while/body/jit(dynamic_update_index_in_dim)/dynamic_update_slice | solution.py:130
  242.0 37.7 %all-gather.1 = bf16[16,1,16]{2,1,0:T(2,128)(2,1)S(1)} all-gather(bf16[1,1,16]{2,1,0:T(2,128)(2,1)S(1)} %bitcast.127), channel_id=1, replica_groups=mesh['seq'=16,'tp'=2] {'seq'}, dimensions={0}, use_global_device_ids=true | all-gather | bytes 544 | tf_op jit(solution)/shard_map/all_gather | solution.py:22
  280.0 2.1 reshape.112
  282.0 33.2 %all-gather.13.cloned.1.call-done = bf16[256,64,128]{2,1,0:T(8,128)(2,1)} async-done(((bf16[16,64,128]{2,1,0:T(8,128)(2,1)}), bf16[256,64,128]{2,1,0:T(8,128)(2,1)}) %all-gather.13.cloned.1.call-update) | async-done | bytes 4194320 | tf_op jit(solution)/shard_map/all_gather | solution.py:22
  315.2 18.3 %while.30 = (s32[]{:T(128)}, f32[16]{0:T(128)S(1)}, f32[16,64,128]{2,1,0:T(8,128)S(1)}, s32[]{:T(128)}, bf16[16,16]{1,0:T(8,128)(2,1)S(1)}, /*index=5*/bf16[16,16,64,128]{3,2,1,0:T(8,128)(2,1)}, s32[]{:T(128)}, s32[]{:T(128)}) while((s32[]{:T(128)}, f32[16]{0:T(128)S(1)}, f32[16,64,128]{2,1,0:T(8,128)S(1)}, s32[]{:T(128)}, ...), condition=%wide.region_6.7_spmd.clone, body=%wide.region_5.6_spmd.clone.sunk | while | flops 655428 | bytes 1311131 | solution.py:35
  315.2 1.1 fusion.87
  316.4 1.1 fusion.87
  317.6 1.1 fusion.87
  318.7 1.1 fusion.87
  319.8 1.1 fusion.87
  321.0 1.1 fusion.87
  322.1 1.1 fusion.87
  323.3 1.1 fusion.87
  324.4 1.1 fusion.87
  325.5 1.1 fusion.87
  326.7 1.1 fusion.87
  327.8 1.1 fusion.87
  329.0 1.1 fusion.87
  330.1 1.1 fusion.87
  331.2 1.1 fusion.87
  334.9 2.5 psum.7
  (95 shorter events, 16.4 us)
Async XLA Ops:
  6.5 15.7 %all-gather.7.cloned.1.call-start = ((), (), s32[]{:S(2)}) async-start(), calls=%async_computation | async-start | bytes 3145728 | tf_op jit(solution)/shard_map/all_gather | solution.py:87
  7.3 79.8 %all-gather.11.cloned.1.call-start = ((), (), s32[]{:S(2)}) async-start(), calls=%async_computation.2 | async-start | bytes 2228224 | tf_op jit(solution)/shard_map/all_gather | solution.py:103
  11.0 190.4 %all-gather.9.cloned.1.call-start = ((), (), s32[]{:S(2)}) async-start(), calls=%async_computation.1 | async-start | bytes 8912896 | tf_op jit(solution)/shard_map/all_gather | solution.py:98
  11.8 303.4 %all-gather.13.cloned.1.call-start = ((), (), s32[]{:S(2)}) async-start(), calls=%async_computation.3 | async-start | bytes 4456448 | tf_op jit(solution)/shard_map/all_gather | solution.py:22
  23.1 43.4 %collective-permute-start = (bf16[3,4096]{1,0:T(4,128)(2,1)S(1)}, bf16[3,4096]{1,0:T(4,128)(2,1)S(1)}, u32[]{:S(2)}, u32[]{:S(2)}) collective-permute-start(bf16[3,4096]{1,0:T(4,128)(2,1)S(1)} %slice.99), channel_id=1, source_target_pairs={{0,2},{2,4},{4,6},{6,8},{8,10},{10,12},{12,14},{14,16},{16,18},{18... | collective-permute-start | bytes 73736 | tf_op jit(solution)/shard_map/ppermute | solution.py:16
  210.0 30.7 %copy-start.1 = (f32[1024]{0:T(1024)S(1)}, f32[1024]{0:T(1024)}, u32[]{:S(2)}) copy-start(f32[1024]{0:T(1024)} %param.27) | copy-start | bytes 12292
  210.0 30.8 %copy-start.2 = (f32[1024]{0:T(1024)S(1)}, f32[1024]{0:T(1024)}, u32[]{:S(2)}) copy-start(f32[1024]{0:T(1024)} %param.25) | copy-start | bytes 12292
  315.2 18.3 %copy-start = (f32[16,64,128]{2,1,0:T(8,128)S(1)}, f32[16,64,128]{2,1,0:T(8,128)}, u32[]{:S(2)}) copy-start(f32[16,64,128]{2,1,0:T(8,128)} %param.26) | copy-start | bytes 1572868
  315.2 18.3 %copy-start.3 = (f32[16]{0:T(128)S(1)}, f32[16]{0:T(128)}, u32[]{:S(2)}) copy-start(f32[16]{0:T(128)} %param.24) | copy-start | bytes 196
Sparse Core Ops, SparseCore 0:
  8.9 13.2 all-gather.6
  25.0 61.9 all-gather.10
  89.8 111.5 all-gather.8
  240.9 74.2 all-gather.12
where the time goes:
time: 347 us; the launch traced here: 345 us
  waiting for transfers between devices  173 us (50%)
  blocking collectives  83.6 us (24%)
  local copies, waits for them, and re-layouts  33.8 us (10%)
  other arithmetic  22.2 us (6%)
  matrix products  15.1 us (4%)
  between operations  13.3 us (4%)
  starting transfers between devices  3.75 us (1%)
    all_gather x1, waiting for transfers between devices, per_device(): lax.all_gather(x_weight, 'seq', axis=0, tiled=True)  111 us
    all_gather x1, blocking collectives, per_device(): lax.all_gather(dt_weight, 'seq', axis=0, tiled=True)  39.7 us
    all_gather x1, blocking collectives, prefix(): lax.all_gather(part.astype(kind), axis)  37.7 us
    all_gather x1, waiting for transfers between devices, prefix(): lax.all_gather(part.astype(kind), axis)  33.2 us
    dynamic_update_slice x2, local copies, waits for them, and re-layouts, per_device(): local_state, local_out = lax.scan(block_update, zero_state, inputs)  26.1 us
    all_gather x1, waiting for transfers between devices, per_device(): lax.all_gather(bc_panel, 'seq', axis=0, tiled=True)  18.1 us
    select_n x32, other arithmetic, turn(): return jax.tree.map(lambda a, b: jnp.where(reached, a, b), new, before)  17.9 us
    all_gather x1, waiting for transfers between devices, per_device(): features = lax.all_gather(tokens, 'tp', axis=1, tiled=True)  8.68 us
  transfers between devices with their start and end apart: 5, of which 4 were waited for; matrix products, arithmetic and copies ran while one was open for 3% of the time, Pallas kernels for 0%

commit v1 on v0

--- a/solution.py
+++ b/solution.py
@@ -1,7 +1,17 @@
+import functools
+
 import jax
 import jax.numpy as jnp
 from jax import lax
+from jax.experimental import pallas as pl
+from jax.experimental.pallas import tpu as pltpu
 from jax.sharding import PartitionSpec as P
+
+MESH = pl.DeviceIdType.MESH
+PLANE = 4
+TAIL = 16
+F32 = jnp.float32
+BF16 = jnp.bfloat16
 
 N = 128
 GROUP = 128
@@ -70,7 +80,7 @@
     return (earlier[0] * later[0], later[0][:, None, None] * earlier[1] + later[1])
 
 
-def per_device(
+def portable(
     tokens,
     x_weight,
     bc_weight,
@@ -154,6 +164,460 @@
     return (normed - penalty[:, None] * steer[None, :]).astype(jnp.bfloat16)
 
 
+def dot(a, b):
+    return jnp.dot(a, b, preferred_element_type=F32)
+
+
+def split_dot(a, b):
+    high = b.astype(BF16)
+    low = (b - high.astype(F32)).astype(BF16)
+    return dot(a, high) + dot(a, low)
+
+
+def gather_kernel(
+    planes, tok_ref, pack_ref, x_out, bc_out, dt_out, xt_out, bct_out,
+    toks, weights, x_keep, bc_keep, x_tail, bc_tail, send_sem, tok_sem, sib_sem, swap_sem, line_sem, tail_sem, own_sem,
+):
+    seq, core = lax.axis_index("seq"), lax.axis_index("tp")
+    plane, member = lax.div(seq, PLANE), lax.rem(seq, PLANE)
+    base = plane * PLANE
+    own_rows, columns = tok_ref.shape
+    half = own_rows // 2
+    depth = pack_ref.shape[1] - TAIL
+    my_x, my_y = lax.rem(member, 2), lax.div(member, 2)
+    members = [member, my_y * 2 + 1 - my_x, (1 - my_y) * 2 + my_x, (1 - my_y) * 2 + 1 - my_x]
+    has_below, has_above = plane > 0, plane < planes - 1
+
+    barrier = pltpu.get_barrier_semaphore()
+
+    def greet(s, c):
+        pl.semaphore_signal(barrier, inc=1, device_id=(s, c), device_id_type=MESH)
+
+    for j in (1, 2, 3):
+        greet(base + members[j], core)
+    greet(seq, 1 - core)
+
+    @pl.when(has_below)
+    def _():
+        greet(seq - PLANE, core)
+        greet(seq - PLANE, 1 - core)
+
+    @pl.when(has_above)
+    def _():
+        greet(seq + PLANE, core)
+        greet(seq + PLANE, 1 - core)
+
+    below, above = jnp.where(has_below, 2, 0), jnp.where(has_above, 2, 0)
+    pl.semaphore_wait(barrier, 4 + below + above)
+
+    started = []
+
+    def send(source, target, sem, device, when=None):
+        copy = pltpu.make_async_remote_copy(
+            src_ref=source, dst_ref=target, send_sem=send_sem.at[len(started)], recv_sem=sem,
+            device_id=device, device_id_type=MESH,
+        )
+        started.append((copy, when))
+        if when is None:
+            copy.start()
+        else:
+            pl.when(when)(lambda: copy.start())
+
+    def arrived(target, sem, when=None):
+        copy = pltpu.make_async_remote_copy(
+            src_ref=target, dst_ref=target, send_sem=send_sem.at[0], recv_sem=sem,
+            device_id=(seq, 1 - core), device_id_type=MESH,
+        )
+        if when is None:
+            copy.wait_recv()
+        else:
+            pl.when(when)(lambda: copy.wait_recv())
+
+    def piece(c, j, h):
+        return toks.at[c, pl.ds(pl.multiple_of(members[j] * own_rows + h * half, half), half)]
+
+    def own_piece(h):
+        return tok_ref.at[pl.ds(h * half, half)]
+
+    def block(p, j):
+        return weights.at[p, members[j]]
+
+    across = [(base + members[j], core) for j in range(4)]
+    up, down, sibling = (seq + PLANE, core), (seq - PLANE, core), (seq, 1 - core)
+
+    own_weights = pltpu.make_async_copy(pack_ref.at[member], block(plane, 0), own_sem.at[0])
+    own_tokens = pltpu.make_async_copy(tok_ref, toks.at[core, pl.ds(pl.multiple_of(member * own_rows, own_rows), own_rows)], own_sem.at[1])
+    own_weights.start()
+    own_tokens.start()
+    for j in (1, 2, 3):
+        send(pack_ref.at[members[j]], weights.at[plane, member], swap_sem.at[j], across[j])
+    send(pack_ref.at[member], block(plane, 0), line_sem.at[0, 1, 0], up, has_above)
+    send(pack_ref.at[member], block(plane, 0), line_sem.at[1, 1, 0], down, has_below)
+    send(own_piece(0), piece(core, 0, 0), tok_sem.at[0], across[1])
+    send(own_piece(1), piece(core, 0, 1), tok_sem.at[2], across[2])
+    send(own_piece(1), piece(core, 0, 1), tok_sem.at[1], across[1])
+    send(own_piece(0), piece(core, 0, 0), tok_sem.at[3], across[2])
+    send(own_piece(0), piece(core, 0, 0), sib_sem.at[0, 0], sibling)
+    send(own_piece(1), piece(core, 0, 1), sib_sem.at[0, 1], sibling)
+    for j in (1, 2, 3):
+        arrived(block(plane, j), swap_sem.at[j])
+        send(block(plane, j), block(plane, j), line_sem.at[0, 1, j], up, has_above)
+        send(block(plane, j), block(plane, j), line_sem.at[1, 1, j], down, has_below)
+
+    def relay(step, j):
+        lower, upper = plane - step, plane + step
+        arrived(block(jnp.maximum(lower, 0), j), line_sem.at[0, step, j], lower >= 0)
+        arrived(block(jnp.minimum(upper, planes - 1), j), line_sem.at[1, step, j], upper < planes)
+        if step < planes - 1:
+            low = block(jnp.maximum(lower, 0), j)
+            high = block(jnp.minimum(upper, planes - 1), j)
+            send(low, low, line_sem.at[0, step + 1, j], up, jnp.logical_and(lower >= 0, has_above))
+            send(high, high, line_sem.at[1, step + 1, j], down, jnp.logical_and(upper < planes, has_below))
+
+    def token(j, h, index, forward=None):
+        here = piece(core, j, h)
+        arrived(here, tok_sem.at[index])
+        if forward is not None:
+            send(here, here, tok_sem.at[forward[0]], across[forward[1]])
+        send(here, here, sib_sem.at[j, h], sibling)
+
+    steps = [(step, j) for step in range(1, planes) for j in range(4)]
+    takes = [
+        (1, 0, 0, (4, 2)), (2, 1, 2, (5, 1)), (1, 1, 1, None), (2, 0, 3, None), (3, 0, 4, None), (3, 1, 5, None),
+    ]
+    places = [3, 3, 7, 7, 11, 11]
+    for at, (step, j) in enumerate(steps):
+        for take, place in zip(takes, places):
+            if place == at:
+                token(*take)
+        relay(step, j)
+    for take, place in zip(takes, places):
+        if place >= len(steps):
+            token(*take)
+    own_weights.wait()
+    own_tokens.wait()
+    for j in range(4):
+        for h in range(2):
+            arrived(piece(1 - core, j, h), sib_sem.at[j, h])
+
+    rows = toks.shape[1]
+    tile = rows // 2
+    channels = x_out.shape[1]
+    per_half = columns // depth
+    filler = jnp.zeros((128 - TAIL, depth), BF16)
+
+    def multiply(at, _):
+        where = pl.ds(pl.multiple_of(at * tile, tile), tile)
+        wide = jnp.zeros((tile, channels + 128), F32)
+        narrow = jnp.zeros((tile, 128), F32)
+        for k in range(2 * per_half):
+            left = toks[k // per_half, where, (k % per_half) * depth : (k % per_half + 1) * depth]
+            wide += dot(left, weights[k // PLANE, k % PLANE, :depth, :])
+            steps_w = jnp.concatenate([weights[k // PLANE, k % PLANE, depth:, :depth], filler], 0)
+            narrow += lax.dot_general(left, steps_w, (((1,), (1,)), ((), ())), preferred_element_type=F32)
+        x_keep[where, :] = wide[:, :channels].astype(BF16)
+        bc_keep[core, where, :] = wide[:, channels:].astype(BF16)
+        dt_out[where, :] = narrow
+        return 0
+
+    lax.fori_loop(0, 2, multiply, 0)
+    last = pl.ds(rows - TAIL, TAIL)
+    send(x_keep.at[last], x_tail, tail_sem.at[0], up, has_above)
+    send(bc_keep.at[core, last], bc_tail.at[core], tail_sem.at[1], up, has_above)
+    send(bc_keep.at[core, last], bc_tail.at[core], tail_sem.at[2], (seq + PLANE, 1 - core), has_above)
+    send(bc_keep.at[core], bc_keep.at[core], tail_sem.at[3], sibling)
+    x_out[...] = x_keep[...]
+
+    @pl.when(jnp.logical_not(has_below))
+    def _():
+        x_tail[...] = jnp.zeros_like(x_tail)
+        bc_tail[...] = jnp.zeros_like(bc_tail)
+
+    arrived(x_tail, tail_sem.at[0], has_below)
+    arrived(bc_tail.at[core], tail_sem.at[1], has_below)
+    arrived(bc_tail.at[1 - core], tail_sem.at[2], has_below)
+    arrived(bc_keep.at[1 - core], tail_sem.at[3])
+    xt_out[...] = x_tail[...]
+    bct_out[...] = bc_tail[...]
+    bc_out[...] = bc_keep[...]
+    for copy, when in started:
+        if when is None:
+            copy.wait_send()
+        else:
+            pl.when(when)(lambda copy=copy: copy.wait_send())
+
+
+def smooth(ref, at, taps):
+    rows = ref[pl.ds(pl.multiple_of(at * GROUP + TAIL - 8, 8), GROUP + 8), :]
+    width = taps.shape[0]
+    summed = taps[0:1, :] * rows[9 - width : 9 - width + GROUP]
+    for k in range(1, width):
+        summed = summed + taps[k : k + 1, :] * rows[9 - width + k : 9 - width + k + GROUP]
+    return (summed / (1.0 + jnp.exp(-summed))).astype(BF16)
+
+
+def spread(values, heads, size):
+    lane = lax.broadcasted_iota(jnp.int32, (values.shape[0], heads * size), 1)
+    wide = jnp.broadcast_to(values[:, heads - 1 : heads], lane.shape)
+    for h in range(heads - 2, -1, -1):
+        wide = jnp.where(lane < (h + 1) * size, values[:, h : h + 1], wide)
+    return wide
+
+
+def layer_kernel(
+    planes, heads, x_ref, bc_ref, dt_ref, xt_ref, bct_ref, taps_x, taps_bc, bias, rate, skip, gain, first, steer, steer_all, out_ref,
+    x_pad, bc_pad, x_conv, bc_conv, s_keep, dt_keep, states, logs, y_keep, state_out, total_out, state_in, total_in,
+    normed, partial, normed_in, partial_in, send_sem, state_sem, total_sem, normed_sem, partial_sem,
+):
+    seq, core = lax.axis_index("seq"), lax.axis_index("tp")
+    plane, member = lax.div(seq, PLANE), lax.rem(seq, PLANE)
+    base = plane * PLANE
+    rows, channels = x_ref.shape
+    size = channels // heads
+    blocks = rows // GROUP
+    per_member = blocks // PLANE
+
+    barrier = pltpu.get_barrier_semaphore()
+    near = [lax.rem(member + j, PLANE) for j in range(PLANE)]
+    far = [lax.rem(plane + j, planes) for j in range(planes)]
+    friends = [(base + near[j], core) for j in range(1, PLANE)] + [(base + near[j], 1 - core) for j in range(PLANE)]
+    friends = friends + [(far[j] * PLANE + member, core) for j in range(1, planes)]
+    for friend in friends:
+        pl.semaphore_signal(barrier, inc=1, device_id=friend, device_id_type=MESH)
+
+    x_pad[0:TAIL, :] = xt_ref[...].astype(F32)
+    x_pad[TAIL:, :] = x_ref[...].astype(F32)
+    for c in range(2):
+        bc_pad[0:TAIL, c * N : (c + 1) * N] = bct_ref[c].astype(F32)
+        bc_pad[TAIL:, c * N : (c + 1) * N] = bc_ref[c].astype(F32)
+    row = lax.broadcasted_iota(jnp.int32, (GROUP, GROUP), 0)
+    column = lax.broadcasted_iota(jnp.int32, (GROUP, GROUP), 1)
+    causal = row >= column
+    lower = causal.astype(BF16)
+
+    def here(at):
+        return pl.ds(pl.multiple_of(at * GROUP, GROUP), GROUP)
+
+    def advance(at, carry):
+        state, log = carry
+        x = smooth(x_pad, at, taps_x[...])
+        bc = smooth(bc_pad, at, taps_bc[...])
+        x_conv[here(at), :] = x
+        bc_conv[here(at), :] = bc
+        raw = dt_ref[here(at), :] + bias[...]
+        dt = jnp.maximum(raw, 0.0) + jnp.log1p(jnp.exp(-jnp.abs(raw)))
+        a = -dt * rate[...]
+        one = a.astype(BF16)
+        rest = a - one.astype(F32)
+        two = rest.astype(BF16)
+        three = (rest - two.astype(F32)).astype(BF16)
+        s = dot(lower, one) + (dot(lower, two) + dot(lower, three))
+        s_keep[here(at), :] = s
+        dt_keep[here(at), :] = dt
+        states[at] = state
+        logs[at] = log
+        end = s[GROUP - 1 : GROUP, :]
+        weight = spread(jnp.exp(end - s) * dt, heads, size)
+        scaled = (x.astype(F32) * weight).astype(BF16)
+        b_turned = bc[:, :N].astype(F32).T.astype(BF16)
+        ended = spread(jnp.broadcast_to(end, (8, GROUP)), heads, size)
+        state = jnp.exp(ended[0:1, :]) * state + dot(b_turned, scaled)
+        return state, log + ended
+
+    state, log = lax.fori_loop(0, blocks, advance, (jnp.zeros((N, channels), F32), jnp.zeros((8, channels), F32)))
+    state_out[...] = state.astype(BF16)
+    total_out[...] = log
+    pl.semaphore_wait(barrier, len(friends))
+
+    started = []
+
+    def remote(source, target, sem, device):
+        return pltpu.make_async_remote_copy(
+            src_ref=source, dst_ref=target, send_sem=send_sem.at[len(started)], recv_sem=sem,
+            device_id=device, device_id_type=MESH,
+        )
+
+    def send(*what):
+        copy = remote(*what)
+        copy.start()
+        started.append(copy)
+
+    for j in range(1, planes):
+        other = (far[j] * PLANE + member, core)
+        send(state_out, state_in.at[planes - j], state_sem.at[planes - j], other)
+        send(total_out, total_in.at[planes - j], total_sem.at[planes - j], other)
+
+    def inside(at, _):
+        x = x_conv[here(at), :]
+        bc = bc_conv[here(at), :]
+        s = s_keep[here(at), :]
+        s_turned = s.T
+        dt_turned = dt_keep[here(at), :].T
+        scores = lax.dot_general(bc[:, N:], bc[:, :N], (((1,), (1,)), ((), ())), preferred_element_type=F32)
+        parts = []
+        for h in range(heads):
+            differ = s[:, h : h + 1] - s_turned[h : h + 1, :]
+            decays = jnp.where(causal, jnp.exp(jnp.where(causal, differ, 0.0)), 0.0)
+            mixing = (scores * decays * dt_turned[h : h + 1, :]).astype(BF16)
+            parts.append(dot(mixing, x[:, h * size : (h + 1) * size]))
+        y_keep[here(at), :] = jnp.concatenate(parts, 1) + skip[...] * x.astype(F32)
+        return 0
+
+    lax.fori_loop(0, blocks, inside, 0)
+
+    for j in range(1, planes):
+        other = (far[j] * PLANE + member, core)
+        remote(state_out, state_in.at[j], state_sem.at[j], other).wait_recv()
+        remote(total_out, total_in.at[j], total_sem.at[j], other).wait_recv()
+    entering = first[...]
+    for j in range(1, planes):
+        later = jnp.exp(total_in[j][0:1, :]) * entering + state_in[j].astype(F32)
+        entering = jnp.where(far[j] < plane, later, entering)
+
+    same = lax.broadcasted_iota(jnp.int32, (channels, channels), 0) // size == lax.broadcasted_iota(jnp.int32, (channels, channels), 1) // size
+    same = same.astype(BF16)
+
+    def finish(at):
+        s = s_keep[here(at), :]
+        c = bc_conv[here(at), :][:, N:]
+        state = states[at] + jnp.exp(logs[at][0:1, :]) * entering
+        y = y_keep[here(at), :] + jnp.exp(spread(s, heads, size)) * split_dot(c, state)
+        square = y * y
+        high = square.astype(BF16)
+        low = (square - high.astype(F32)).astype(BF16)
+        mean = (dot(high, same) + dot(low, same)) * (1.0 / size)
+        scaled = y * lax.rsqrt(mean + EPSILON) * gain[...]
+        normed[here(at), :] = scaled.astype(BF16)
+        along = jnp.sum(scaled * steer[...], axis=1, keepdims=True)
+        partial[at] = jnp.broadcast_to(along, (GROUP, GROUP)).T[0:8, :]
+
+    own_rows = rows // PLANE
+    for j in list(range(1, PLANE)) + [0]:
+        target = near[j]
+        lax.fori_loop(0, per_member, lambda i, _: (finish(target * per_member + i), 0)[1], 0)
+        pieces = partial.at[pl.ds(target * per_member, per_member)]
+        back = (PLANE - j) % PLANE
+        if j:
+            chunk = normed.at[pl.ds(pl.multiple_of(target * own_rows, own_rows), own_rows)]
+            send(chunk, normed_in.at[member], normed_sem.at[back], (base + target, core))
+            send(pieces, partial_in.at[0, back], partial_sem.at[0, back], (base + target, core))
+        send(pieces, partial_in.at[1, back], partial_sem.at[1, back], (base + target, 1 - core))
+    mine = pl.ds(pl.multiple_of(member * own_rows, own_rows), own_rows)
+    normed_in[member] = normed[mine, :]
+    penalty = partial[pl.ds(member * per_member, per_member)]
+    for j in range(PLANE):
+        other = (base + near[j], 1 - core)
+        pieces = partial.at[pl.ds(member * per_member, per_member)]
+        if j:
+            remote(normed.at[mine], normed_in.at[near[j]], normed_sem.at[j], other).wait_recv()
+            remote(pieces, partial_in.at[0, j], partial_sem.at[0, j], other).wait_recv()
+            penalty = penalty + partial_in[0, j]
+        remote(pieces, partial_in.at[1, j], partial_sem.at[1, j], other).wait_recv()
+        penalty = penalty + partial_in[1, j]
+    penalty = penalty * (1.0 / (channels * PLANE * lax.axis_size("tp")) ** 0.5)
+    for i in range(per_member):
+        turned = jnp.broadcast_to(penalty[i][0:1, :], (GROUP, GROUP)).T
+        turned = jnp.concatenate([turned] * (channels // GROUP), 1)
+        span = pl.ds(i * GROUP, GROUP)
+        for j in range(PLANE):
+            value = normed_in[j, span, :].astype(F32) - turned * steer_all[:, j * channels : (j + 1) * channels]
+            out_ref[j, span, :] = value.astype(BF16)
+    for copy in started:
+        copy.wait_send()
+
+
+def per_device(tokens, x_weight, bc_weight, dt_weight, conv_x, conv_bc, dt_bias, decay_rate, d_skip, norm_gain, initial_state, steer):
+    planes = lax.axis_size("seq") // PLANE
+    member = lax.rem(lax.axis_index("seq"), PLANE)
+    own_rows, columns = tokens.shape
+    depth, all_channels = x_weight.shape
+    all_heads = dt_weight.shape[1]
+    channels, heads = all_channels // PLANE, all_heads // PLANE
+    size = channels // heads
+    rows = own_rows * PLANE
+    blocks = rows // GROUP
+
+    steps_w = dt_weight.T.reshape(PLANE, heads, depth)
+    steps_w = jnp.pad(steps_w, ((0, 0), (0, TAIL - heads), (0, channels + 128 - depth)))
+    wide = x_weight.reshape(depth, PLANE, channels).transpose(1, 0, 2)
+    wide = jnp.concatenate([wide, jnp.broadcast_to(bc_weight[None], (PLANE,) + bc_weight.shape)], 2)
+    pack = jnp.concatenate([wide, steps_w], 1)
+
+    vmem = pl.BlockSpec(memory_space=pltpu.VMEM)
+    anywhere = pl.BlockSpec(memory_space=pl.ANY)
+    shape = jax.ShapeDtypeStruct
+    dma = pltpu.SemaphoreType.DMA
+    x_pre, bc_pre, dt_raw, x_tail, bc_tail = pl.pallas_call(
+        functools.partial(gather_kernel, planes),
+        out_shape=(
+            shape((rows, channels), BF16), shape((2, rows, 128), BF16), shape((rows, 128), F32),
+            shape((TAIL, channels), BF16), shape((2, TAIL, 128), BF16),
+        ),
+        in_specs=[anywhere, anywhere],
+        out_specs=[vmem] * 5,
+        scratch_shapes=[
+            pltpu.VMEM((2, rows, columns), BF16),
+            pltpu.VMEM((planes, PLANE, depth + TAIL, channels + 128), BF16),
+            pltpu.VMEM((rows, channels), BF16),
+            pltpu.VMEM((2, rows, 128), BF16),
+            pltpu.VMEM((TAIL, channels), BF16),
+            pltpu.VMEM((2, TAIL, 128), BF16),
+            dma((23 + 8 * planes,)),
+            dma((6,)),
+            dma((4, 2)),
+            dma((4,)),
+            dma((2, planes, 4)),
+            dma((4,)),
+            dma((2,)),
+        ],
+        compiler_params=pltpu.CompilerParams(collective_id=0, has_side_effects=True, vmem_limit_bytes=48 * 2**20),
+    )(tokens, pack)
+
+    def mine(value, axis=0):
+        count = value.shape[axis] // PLANE
+        return lax.dynamic_slice_in_dim(value, member * count, count, axis)
+
+    def lanes(value):
+        return jnp.pad(mine(value), (0, 128 - heads))[None, :]
+
+    first = mine(initial_state).reshape(channels, N).T
+    out = pl.pallas_call(
+        functools.partial(layer_kernel, planes, heads),
+        out_shape=shape((PLANE, own_rows, channels), BF16),
+        in_specs=[vmem] * 14,
+        out_specs=vmem,
+        scratch_shapes=[
+            pltpu.VMEM((rows + TAIL, channels), F32),
+            pltpu.VMEM((rows + TAIL, 2 * N), F32),
+            pltpu.VMEM((rows, channels), BF16),
+            pltpu.VMEM((rows, 2 * N), BF16),
+            pltpu.VMEM((rows, 128), F32),
+            pltpu.VMEM((rows, 128), F32),
+            pltpu.VMEM((blocks, N, channels), F32),
+            pltpu.VMEM((blocks, 8, channels), F32),
+            pltpu.VMEM((rows, channels), F32),
+            pltpu.VMEM((N, channels), BF16),
+            pltpu.VMEM((8, channels), F32),
+            pltpu.VMEM((planes, N, channels), BF16),
+            pltpu.VMEM((planes, 8, channels), F32),
+            pltpu.VMEM((rows, channels), BF16),
+            pltpu.VMEM((blocks, 8, GROUP), F32),
+            pltpu.VMEM((PLANE, own_rows, channels), BF16),
+            pltpu.VMEM((2, PLANE, blocks // PLANE, 8, GROUP), F32),
+            dma((2 * planes + 3 * PLANE,)),
+            dma((planes,)),
+            dma((planes,)),
+            dma((PLANE,)),
+            dma((2, PLANE)),
+        ],
+        compiler_params=pltpu.CompilerParams(collective_id=1, has_side_effects=True, vmem_limit_bytes=48 * 2**20),
+    )(
+        x_pre, bc_pre, dt_raw, x_tail, bc_tail, mine(conv_x, 1), conv_bc, lanes(dt_bias), lanes(decay_rate),
+        jnp.repeat(mine(d_skip), size)[None, :], mine(norm_gain)[None, :], first, mine(steer)[None, :], steer[None, :],
+    )
+    return out.transpose(1, 0, 2).reshape(own_rows, all_channels)
+
+
 def solution(mesh):
     placed = (
         P("seq", "tp"),
@@ -169,6 +633,7 @@
         P("tp", None, None),
         P("tp"),
     )
+    planar = mesh.shape["tp"] == 2 and mesh.shape["seq"] % PLANE == 0
     return jax.shard_map(
-        per_device, mesh=mesh, in_specs=placed, out_specs=P("seq", "tp"), check_vma=False
-    )
+        per_device if planar else portable, mesh=mesh, in_specs=placed, out_specs=P("seq", "tp"), check_vma=False
+    )

time: 347 us -> 101 us (0.29)
  waiting for transfers between devices: 173 us -> 0 us
  Pallas kernels: 0 us -> 93.1 us
  blocking collectives: 83.6 us -> 0 us
  local copies, waits for them, and re-layouts: 33.8 us -> 6.56 us
  other arithmetic: 22.2 us -> 0.14 us
  matrix products: 15.1 us -> 0 us
  between operations: 13.3 us -> 0.11 us
  starting transfers between devices: 3.75 us -> 0 us
    all_gather x4 -> x0, waiting for transfers between devices: 171 us -> none  [the longest x1 111 us: per_device(): lax.all_gather(x_weight, 'seq', axis=0, tiled=True)]
    pallas_call x0 -> x2, Pallas kernels: none -> 93.1 us  [the longest x1 70.9 us: per_device(): pl.pallas_call(functools.partial(gather_kernel, planes), out_shape=(shape...]
    all_gather x3 -> x0, blocking collectives: 81.1 us -> none  [the longest x1 39.7 us: per_device(): lax.all_gather(dt_weight, 'seq', axis=0, tiled=True)]
    dynamic_update_slice x2 -> x0, local copies, waits for them, and re-layouts: 26.1 us -> none  [per_device(): local_state, local_out = lax.scan(block_update, zero_state, inputs)]
    select_n x32 -> x0, other arithmetic: 17.9 us -> none  [turn(): return jax.tree.map(lambda a, b: jnp.where(reached, a, b), new, before)]
    dot_general x12 -> x0, matrix products: 15.1 us -> none  [the longest x1 6.43 us: per_device(): jnp.dot(source, lax.all_gather(x_weight, 'seq', axis=0, tiled=True), pref...]
    ppermute x1 -> x0, starting transfers between devices: 3.63 us -> none  [passed_along(): lax.ppermute(value, axis, [(source, source + steps) for source in range(f...]
  transfers between devices with their start and end apart: 5 -> 0, of which waited for: 4 -> 0; matrix products, arithmetic and copies ran while one was open for 3% -> 0% of each run, Pallas kernels for 0% -> 0%
where the time goes in v1:
time: 101 us; the launch traced here: 99.9 us
  Pallas kernels  93.1 us (92%)
  local copies, waits for them, and re-layouts  6.56 us (6%)
    pallas_call x1, Pallas kernels, per_device(): pl.pallas_call(functools.partial(gather_kernel, planes), out_shape=(shape...  70.9 us
    pallas_call x1, Pallas kernels, per_device(): pl.pallas_call(functools.partial(layer_kernel, planes, heads), out_shape=...  22.2 us
    unnamed x17, local copies, waits for them, and re-layouts  2.34 us

profile of v1, /device:TPU:0, one launch (start us, length us, event | category | flops | bytes accessed | tf_op | source)
XLA Modules:
  0.0 99.9 jit_solution(12465470209840350800)
XLA Ops:
  0.0 0.0 copy-start
  0.0 0.8 reshape.14
  0.8 0.0 copy-start.4
  0.8 1.3 %copy.14 = bf16[256,1024]{0,1:T(8,128)(2,1)S(1)} copy(bf16[256,1024]{1,0:T(8,128)(2,1)} %param.13) | data formatting | bytes 1048576 | tf_op args[1]
  2.0 0.2 copy.15
  2.3 0.0 copy-start.1
  2.3 0.0 copy-done.4
  2.3 0.1 fusion.1.pack_ref
  2.5 1.0 %copy-done.1 = bf16[256,2048]{1,0:T(8,128)(2,1)S(1)} copy-done((bf16[256,2048]{1,0:T(8,128)(2,1)S(1)}, bf16[256,2048]{1,0:T(8,128)(2,1)}, u32[]{:S(2)}) %copy-start.1) | copy-done | bytes 1048600
  3.5 0.0 copy-start.5
  3.5 0.0 copy-start.6
  3.5 0.0 copy-start.7
  3.5 0.0 copy-start.3
  3.5 70.9 %shard_map.118 = (bf16[1024,256]{1,0:T(8,128)(2,1)S(1)}, bf16[2,1024,128]{2,1,0:T(8,128)(2,1)S(1)}, f32[1024,128]{1,0:T(8,128)S(1)}, bf16[16,256]{1,0:T(8,128)(2,1)S(1)}, bf16[2,16,128]{2,1,0:T(8,128)(2,1)S(1)}) custom-call(bf16[256,2048]{1,0:T(8,128)(2,1)S(1)} %copy-done.1, bf16[4,272,384]{2,1,0:T(8,128)(2,1)S(1)} %fusion.1.pack_ref), custom_call_target="tpu_custom_call" | custom-call | tf_op jit(solution)/shard_map/pallas_call | solution.py:550
  74.4 0.7 constant_dynamic-slice_fusion.1.taps_x
  75.1 0.0 copy-done.5
  75.1 0.1 dynamic_slice.23
  75.2 0.0 copy-done.6
  75.2 0.1 dynamic_slice.22
  75.3 0.0 copy-done.7
  75.3 0.1 dynamic_slice.24
  75.4 0.1 broadcast_in_dim.27
  75.4 0.1 broadcast_in_dim_reshape.3.skip
  75.5 0.8 dynamic_slice.25
  76.3 0.0 copy-done
  76.3 0.1 copy.16
  76.4 0.0 copy-done.2
  76.4 0.1 dynamic_slice.27
  76.5 0.0 copy-done.3
  76.5 22.2 %shard_map.119 = bf16[4,256,256]{2,1,0:T(8,128)(2,1)S(1)} custom-call(bf16[1024,256]{1,0:T(8,128)(2,1)S(1)} %get-tuple-element.10.x_ref, bf16[2,1024,128]{2,1,0:T(8,128)(2,1)S(1)} %get-tuple-element.11.bc_ref, f32[1024,128]{1,0:T(8,128)S(1)} %get-tuple-element.12.dt_ref, bf16[16,256]{1,0:T(8,128)(2,1)S(1)} %get-tuple-element.13.xt_ref, ...), custom_call_target="tpu_custom_call" | custom-call | tf_op jit(solution)/shard_map/pallas_call | solution.py:584
  98.7 0.2 copy.17
  98.9 1.0 %copy.18 = bf16[256,1024]{1,0:T(8,128)(2,1)} copy(bf16[256,1024]{0,1:T(8,128)(2,1)S(1)} %bitcast.20) | data formatting | bytes 1048576 | tf_op jit(solution)/shard_map/reshape | solution.py:618
  (4 shorter events, 0.0 us)
Async XLA Ops:
  0.0 76.3 %copy-start = (f32[16,64,128]{2,1,0:T(8,128)S(1)}, f32[16,64,128]{2,1,0:T(8,128)}, u32[]{:S(2)}) copy-start(f32[16,64,128]{2,1,0:T(8,128)} %param.22) | copy-start | bytes 1572868
  0.8 1.5 %copy-start.4 = (bf16[256,128]{1,0:T(8,128)(2,1)S(1)}, bf16[256,128]{1,0:T(8,128)(2,1)}, u32[]{:S(2)}) copy-start(bf16[256,128]{1,0:T(8,128)(2,1)} %param.14) | copy-start | bytes 196612
  2.3 1.2 %copy-start.1 = (bf16[256,2048]{1,0:T(8,128)(2,1)S(1)}, bf16[256,2048]{1,0:T(8,128)(2,1)}, u32[]{:S(2)}) copy-start(bf16[256,2048]{1,0:T(8,128)(2,1)} %tok_ref.1) | copy-start | bytes 3145732
  3.5 71.6 %copy-start.5 = (f32[16]{0:T(128)S(1)}, f32[16]{0:T(128)}, u32[]{:S(2)}) copy-start(f32[16]{0:T(128)} %param.19) | copy-start | bytes 196
  3.5 71.7 %copy-start.6 = (f32[16]{0:T(128)S(1)}, f32[16]{0:T(128)}, u32[]{:S(2)}) copy-start(f32[16]{0:T(128)} %param.18) | copy-start | bytes 196
  3.5 71.8 %copy-start.7 = (f32[16]{0:T(128)S(1)}, f32[16]{0:T(128)}, u32[]{:S(2)}) copy-start(f32[16]{0:T(128)} %param.20) | copy-start | bytes 196
  3.5 72.9 %copy-start.2 = (f32[1024]{0:T(1024)S(1)}, f32[1024]{0:T(1024)}, u32[]{:S(2)}) copy-start(f32[1024]{0:T(1024)} %param.23) | copy-start | bytes 12292
  3.5 73.0 %copy-start.3 = (f32[4,256]{1,0:T(4,128)S(1)}, f32[4,256]{1,0:T(4,128)}, u32[]{:S(2)}) copy-start(f32[4,256]{1,0:T(4,128)} %taps_bc.1) | copy-start | bytes 12292

commit v2 on v0

--- a/solution.py
+++ b/solution.py
@@ -1,7 +1,17 @@
+import functools
+
 import jax
 import jax.numpy as jnp
 from jax import lax
+from jax.experimental import pallas as pl
+from jax.experimental.pallas import tpu as pltpu
 from jax.sharding import PartitionSpec as P
+
+MESH = pl.DeviceIdType.MESH
+PLANE = 4
+TAIL = 16
+F32 = jnp.float32
+BF16 = jnp.bfloat16
 
 N = 128
 GROUP = 128
@@ -70,7 +80,7 @@
     return (earlier[0] * later[0], later[0][:, None, None] * earlier[1] + later[1])
 
 
-def per_device(
+def portable(
     tokens,
     x_weight,
     bc_weight,
@@ -154,6 +164,471 @@
     return (normed - penalty[:, None] * steer[None, :]).astype(jnp.bfloat16)
 
 
+def dot(a, b):
+    return jnp.dot(a, b, preferred_element_type=F32)
+
+
+def split_dot(a, b):
+    high = b.astype(BF16)
+    low = (b - high.astype(F32)).astype(BF16)
+    return dot(a, high) + dot(a, low)
+
+
+def smooth(ref, at, taps):
+    rows = ref[pl.ds(pl.multiple_of(at * GROUP + TAIL - 8, 8), GROUP + 8), :]
+    width = taps.shape[0]
+    summed = taps[0:1, :] * rows[9 - width : 9 - width + GROUP]
+    for k in range(1, width):
+        summed = summed + taps[k : k + 1, :] * rows[9 - width + k : 9 - width + k + GROUP]
+    return (summed / (1.0 + jnp.exp(-summed))).astype(BF16)
+
+
+def spread(values, heads, size):
+    lane = lax.broadcasted_iota(jnp.int32, (values.shape[0], heads * size), 1)
+    wide = jnp.broadcast_to(values[:, heads - 1 : heads], lane.shape)
+    for h in range(heads - 2, -1, -1):
+        wide = jnp.where(lane < (h + 1) * size, values[:, h : h + 1], wide)
+    return wide
+
+
+def layer_kernel(
+    planes, heads, tok_ref, xw_ref, pack_ref, taps_x, taps_bc, small, gain, first, steer, out_ref,
+    toks, weights, wide, narrow, x_tail, x_last, bc_own, bc_all, bc_tail,
+    x_pad, bc_pad, x_conv, bc_conv, s_keep, dt_keep, states, logs, y_keep, state_out, total_out, state_in, total_in,
+    normed, partial, normed_in, partial_in,
+    send_sem, tok_sem, sib_sem, swap_sem, line_sem, own_sem, tail_sem, bct_sem, bc_sem, state_sem, total_sem, normed_sem, partial_sem,
+):
+    seq, core = lax.axis_index("seq"), lax.axis_index("tp")
+    plane, member = lax.div(seq, PLANE), lax.rem(seq, PLANE)
+    base = plane * PLANE
+    own_rows, columns = tok_ref.shape
+    rows = own_rows * PLANE
+    half = own_rows // 2
+    depth = xw_ref.shape[0]
+    channels = weights.shape[3]
+    size = channels // heads
+    quarter = weights.shape[2] - depth - TAIL
+    blocks = rows // GROUP
+    per_member = blocks // PLANE
+    my_x, my_y = lax.rem(member, 2), lax.div(member, 2)
+
+    def member_at(j):
+        return lax.rem(my_y + j // 2, 2) * 2 + lax.rem(my_x + j % 2, 2)
+
+    members = [member_at(j) for j in range(PLANE)]
+    far = [lax.rem(plane + j, planes) for j in range(planes)]
+    has_below, has_above = plane > 0, plane < planes - 1
+
+    barrier = pltpu.get_barrier_semaphore()
+
+    def greet(s, c):
+        pl.semaphore_signal(barrier, inc=1, device_id=(s, c), device_id_type=MESH)
+
+    for j in range(PLANE):
+        greet(base + members[j], 1 - core)
+        if j:
+            greet(base + members[j], core)
+
+    @pl.when(has_below)
+    def _():
+        for m in range(PLANE):
+            for c in range(2):
+                greet(base - PLANE + m, c)
+
+    @pl.when(has_above)
+    def _():
+        for m in range(PLANE):
+            for c in range(2):
+                greet(base + PLANE + m, c)
+
+    greeted = 2 * PLANE - 1 + jnp.where(has_below, 2 * PLANE, 0) + jnp.where(has_above, 2 * PLANE, 0)
+    for j in range(1, planes):
+        distant = jnp.abs(far[j] - plane) > 1
+        pl.when(distant)(lambda j=j: greet(far[j] * PLANE + member, core))
+        greeted = greeted + jnp.where(distant, 1, 0)
+    pl.semaphore_wait(barrier, greeted)
+
+    started = []
+
+    def send(source, target, sem, device, when=None):
+        copy = pltpu.make_async_remote_copy(
+            src_ref=source, dst_ref=target, send_sem=send_sem.at[len(started)], recv_sem=sem,
+            device_id=device, device_id_type=MESH,
+        )
+        started.append((copy, when))
+        if when is None:
+            copy.start()
+        else:
+            pl.when(when)(lambda: copy.start())
+
+    def arrived(target, sem, when=None):
+        copy = pltpu.make_async_remote_copy(
+            src_ref=target, dst_ref=target, send_sem=send_sem.at[0], recv_sem=sem,
+            device_id=(seq, 1 - core), device_id_type=MESH,
+        )
+        if when is None:
+            copy.wait_recv()
+        else:
+            pl.when(when)(lambda: copy.wait_recv())
+
+    def piece(c, j, h):
+        return toks.at[c, pl.ds(pl.multiple_of(members[j] * own_rows + h * half, half), half)]
+
+    def own_piece(h):
+        return tok_ref.at[pl.ds(h * half, half)]
+
+    def block(p, j):
+        return weights.at[p, members[j]]
+
+    across = [(base + members[j], core) for j in range(PLANE)]
+    up, down, sibling = (seq + PLANE, core), (seq - PLANE, core), (seq, 1 - core)
+
+    def quarter_of(m):
+        return xw_ref.at[:, pl.ds(pl.multiple_of(m * channels, channels), channels)]
+
+    def both(m, slot, sem, device, when=None):
+        send(quarter_of(m), weights.at[plane, slot, pl.ds(0, depth)], sem, device, when)
+        send(pack_ref.at[m], weights.at[plane, slot, pl.ds(depth, quarter + TAIL)], sem, device, when)
+
+    own_copies = [
+        pltpu.make_async_copy(quarter_of(member), weights.at[plane, member, pl.ds(0, depth)], own_sem.at[0]),
+        pltpu.make_async_copy(pack_ref.at[member], weights.at[plane, member, pl.ds(depth, quarter + TAIL)], own_sem.at[1]),
+        pltpu.make_async_copy(tok_ref, toks.at[core, pl.ds(pl.multiple_of(member * own_rows, own_rows), own_rows)], own_sem.at[2]),
+    ]
+    for copy in own_copies:
+        copy.start()
+    for j in (1, 2, 3):
+        both(members[j], member, swap_sem.at[j], across[j])
+    both(member, member, line_sem.at[0, 1, 0], up, has_above)
+    both(member, member, line_sem.at[1, 1, 0], down, has_below)
+    send(own_piece(0), piece(core, 0, 0), tok_sem.at[0], across[1])
+    send(own_piece(1), piece(core, 0, 1), tok_sem.at[2], across[2])
+    send(own_piece(1), piece(core, 0, 1), tok_sem.at[1], across[1])
+    send(own_piece(0), piece(core, 0, 0), tok_sem.at[3], across[2])
+    send(own_piece(0), piece(core, 0, 0), sib_sem.at[0, 0], sibling)
+    send(own_piece(1), piece(core, 0, 1), sib_sem.at[0, 1], sibling)
+    for j in (1, 2, 3):
+        arrived(block(plane, j), swap_sem.at[j])
+        send(block(plane, j), block(plane, j), line_sem.at[0, 1, j], up, has_above)
+        send(block(plane, j), block(plane, j), line_sem.at[1, 1, j], down, has_below)
+
+    def relay(step, j):
+        lower, upper = plane - step, plane + step
+        arrived(block(jnp.maximum(lower, 0), j), line_sem.at[0, step, j], lower >= 0)
+        arrived(block(jnp.minimum(upper, planes - 1), j), line_sem.at[1, step, j], upper < planes)
+        if step < planes - 1:
+            low = block(jnp.maximum(lower, 0), j)
+            high = block(jnp.minimum(upper, planes - 1), j)
+            send(low, low, line_sem.at[0, step + 1, j], up, jnp.logical_and(lower >= 0, has_above))
+            send(high, high, line_sem.at[1, step + 1, j], down, jnp.logical_and(upper < planes, has_below))
+
+    def token(j, h, index, forward=None):
+        here = piece(core, j, h)
+        arrived(here, tok_sem.at[index])
+        if forward is not None:
+            send(here, here, tok_sem.at[forward[0]], across[forward[1]])
+        send(here, here, sib_sem.at[j, h], sibling)
+
+    def from_sibling(j):
+        for h in range(2):
+            arrived(piece(1 - core, j, h), sib_sem.at[j, h])
+
+    filler = jnp.zeros((128 - quarter - TAIL, depth), BF16)
+
+    def multiply(j, p):
+        where = pl.ds(pl.multiple_of(member_at(j) * own_rows, own_rows), own_rows)
+        per_core = columns // (PLANE * depth)
+        side = p // per_core
+        total_wide, total_narrow = wide[where, :], narrow[where, :]
+        for k in range(PLANE):
+            span = pl.ds(pl.multiple_of((p % per_core) * (PLANE * depth) + k * depth, depth), depth)
+            left = toks[side, where, span]
+            total_wide += dot(left, weights[p, k, 0:depth, :])
+            turned = jnp.concatenate([weights[p, k, depth:, :], filler], 0)
+            total_narrow += lax.dot_general(left, turned, (((1,), (1,)), ((), ())), preferred_element_type=F32)
+        wide[where, :] = total_wide
+        narrow[where, :] = total_narrow
+
+    def multiply_all(parts, lowest, highest):
+        first_part, last_part = parts
+
+        def at(j, _):
+            return lax.fori_loop(lowest, highest, lambda p, _: (multiply(j, p), 0)[1], 0)
+
+        lax.fori_loop(first_part, last_part, at, 0)
+
+    wide[...] = jnp.zeros_like(wide)
+    narrow[...] = jnp.zeros_like(narrow)
+    takes = [
+        (1, 0, 0, (4, 2)), (2, 1, 2, (5, 1)), (1, 1, 1, None), (2, 0, 3, None),
+    ]
+    places = [3, 3, 6, 6]
+    near_low, near_high = jnp.maximum(plane - (planes - 2), 0), jnp.minimum(plane + planes - 1, planes)
+    steps = [(step, j) for step in range(1, planes) for j in range(PLANE)]
+    for at, (step, j) in enumerate(steps):
+        for take, place in zip(takes, places):
+            if min(place, len(steps) - 1) == at:
+                token(*take)
+        if at == len(steps) - PLANE + 1:
+            for copy in own_copies:
+                copy.wait()
+            for i in range(3):
+                from_sibling(i)
+            multiply_all((0, 3), near_low, near_high)
+        relay(step, j)
+    token(3, 0, 4)
+    token(3, 1, 5)
+    multiply_all((0, 3), 0, near_low)
+    multiply_all((0, 3), near_high, planes)
+    from_sibling(3)
+    multiply_all((3, 4), 0, planes)
+
+    x_last[...] = wide[rows - TAIL : rows, :].astype(BF16)
+    send(x_last, x_tail, tail_sem, up, has_above)
+    me = core * PLANE + member
+    for i in range(PLANE):
+        part = rows // PLANE
+        bc_own[:, i * part : (i + 1) * part] = narrow[i * part : (i + 1) * part, :].T[0:quarter, :].astype(BF16)
+    for j in range(PLANE):
+        for c in (core, 1 - core):
+            if j or c is not core:
+                send(bc_own, bc_all.at[me], bc_sem.at[me], (base + members[j], c))
+    last = bc_own.at[:, pl.ds(rows - GROUP, GROUP)]
+    for m in range(PLANE):
+        for c in range(2):
+            send(last, bc_tail.at[me], bct_sem.at[me], (base + PLANE + m, c), has_above)
+    bc_all[me] = bc_own[...]
+
+    mine = pl.ds(pl.multiple_of(member * channels, channels), channels)
+    own_small = pltpu.roll(small[...], lax.rem(128 - member * heads, 128), 1)
+    bias, rate = own_small[0:1, :], own_small[1:2, :]
+    skip = spread(own_small, heads, size)[2:3, :]
+    taps = taps_x[:, mine]
+    own_gain, own_steer = gain[:, mine], steer[:, mine]
+    row = lax.broadcasted_iota(jnp.int32, (GROUP, GROUP), 0)
+    column = lax.broadcasted_iota(jnp.int32, (GROUP, GROUP), 1)
+    causal = row >= column
+    lower = causal.astype(BF16)
+
+    def here(at):
+        return pl.ds(pl.multiple_of(at * GROUP, GROUP), GROUP)
+
+    def steps_of(at, _):
+        raw = pltpu.roll(narrow[here(at), :], 128 - quarter, 1) + bias
+        dt = jnp.maximum(raw, 0.0) + jnp.log1p(jnp.exp(-jnp.abs(raw)))
+        a = -dt * rate
+        one = a.astype(BF16)
+        rest = a - one.astype(F32)
+        two = rest.astype(BF16)
+        three = (rest - two.astype(F32)).astype(BF16)
+        s_keep[here(at), :] = dot(lower, one) + (dot(lower, two) + dot(lower, three))
+        dt_keep[here(at), :] = dt
+        x_pad[pl.ds(pl.multiple_of(at * GROUP + TAIL, TAIL), GROUP), :] = wide[here(at), :].astype(BF16).astype(F32)
+        return 0
+
+    lax.fori_loop(0, blocks, steps_of, 0, unroll=2)
+
+    @pl.when(jnp.logical_not(has_below))
+    def _():
+        x_tail[...] = jnp.zeros_like(x_tail)
+        bc_tail[...] = jnp.zeros_like(bc_tail)
+
+    arrived(x_tail, tail_sem, has_below)
+    x_pad[0:TAIL, :] = x_tail[...].astype(F32)
+
+    def convolved(at, _):
+        x_conv[here(at), :] = smooth(x_pad, at, taps)
+        return 0
+
+    lax.fori_loop(0, blocks, convolved, 0, unroll=2)
+
+    for j in range(PLANE):
+        for c in (core, 1 - core):
+            if j or c is not core:
+                sender = c * PLANE + members[j]
+                arrived(bc_all.at[sender], bc_sem.at[sender])
+    for sender in range(2 * PLANE):
+        arrived(bc_tail.at[sender], bct_sem.at[sender], has_below)
+    bc_pad[0:TAIL, :] = bc_tail[...].astype(F32).reshape(2 * N, GROUP).T[GROUP - TAIL :, :]
+
+    def unturned(at, _):
+        turned = bc_all[:, :, here(at)].astype(F32).reshape(2 * N, GROUP)
+        bc_pad[pl.ds(pl.multiple_of(at * GROUP + TAIL, TAIL), GROUP), :] = turned.T
+        return 0
+
+    lax.fori_loop(0, blocks, unturned, 0, unroll=2)
+
+    def advance(at, carry):
+        state, log = carry
+        bc = smooth(bc_pad, at, taps_bc[...])
+        bc_conv[here(at), :] = bc
+        s = s_keep[here(at), :]
+        states[at] = state
+        logs[at] = log
+        end = s[GROUP - 1 : GROUP, :]
+        weight = spread(jnp.exp(end - s) * dt_keep[here(at), :], heads, size)
+        scaled = (x_conv[here(at), :].astype(F32) * weight).astype(BF16)
+        b_turned = bc[:, :N].astype(F32).T.astype(BF16)
+        ended = spread(jnp.broadcast_to(end, (8, GROUP)), heads, size)
+        state = jnp.exp(ended[0:1, :]) * state + dot(b_turned, scaled)
+        return state, log + ended
+
+    zeros = (jnp.zeros((N, channels), F32), jnp.zeros((8, channels), F32))
+    state, log = lax.fori_loop(0, blocks, advance, zeros, unroll=2)
+    state_out[...] = state.astype(BF16)
+    total_out[...] = log
+    for j in range(1, planes):
+        other = (far[j] * PLANE + member, core)
+        send(state_out, state_in.at[planes - j], state_sem.at[planes - j], other)
+        send(total_out, total_in.at[planes - j], total_sem.at[planes - j], other)
+
+    def inside(at, _):
+        x = x_conv[here(at), :]
+        bc = bc_conv[here(at), :]
+        s = s_keep[here(at), :]
+        s_turned = s.T
+        dt_turned = dt_keep[here(at), :].T
+        scores = lax.dot_general(bc[:, N:], bc[:, :N], (((1,), (1,)), ((), ())), preferred_element_type=F32)
+        parts = []
+        for h in range(heads):
+            differ = s[:, h : h + 1] - s_turned[h : h + 1, :]
+            decays = jnp.where(causal, jnp.exp(jnp.where(causal, differ, 0.0)), 0.0)
+            mixing = (scores * decays * dt_turned[h : h + 1, :]).astype(BF16)
+            parts.append(dot(mixing, x[:, h * size : (h + 1) * size]))
+        y_keep[here(at), :] = jnp.concatenate(parts, 1) + skip * x.astype(F32)
+        return 0
+
+    lax.fori_loop(0, blocks, inside, 0, unroll=2)
+
+    entering = first[pl.ds(pl.multiple_of(member * channels, channels), channels), :].T
+    for j in range(1, planes):
+        arrived(state_in.at[j], state_sem.at[j])
+        arrived(total_in.at[j], total_sem.at[j])
+    for j in range(1, planes):
+        later = jnp.exp(total_in[j][0:1, :]) * entering + state_in[j].astype(F32)
+        entering = jnp.where(far[j] < plane, later, entering)
+
+    group_of = lax.broadcasted_iota(jnp.int32, (2, channels, channels), 1) // size
+    same = (group_of[0] == lax.broadcasted_iota(jnp.int32, (channels, channels), 1) // size).astype(BF16)
+
+    def finish(at):
+        s = s_keep[here(at), :]
+        c = bc_conv[here(at), :][:, N:]
+        state = states[at] + jnp.exp(logs[at][0:1, :]) * entering
+        y = y_keep[here(at), :] + jnp.exp(spread(s, heads, size)) * split_dot(c, state)
+        square = y * y
+        high = square.astype(BF16)
+        low = (square - high.astype(F32)).astype(BF16)
+        mean = (dot(high, same) + dot(low, same)) * (1.0 / size)
+        scaled = y * lax.rsqrt(mean + EPSILON) * own_gain
+        normed[here(at), :] = scaled.astype(BF16)
+        along = jnp.sum(scaled * own_steer, axis=1, keepdims=True)
+        partial[at] = jnp.broadcast_to(along, (GROUP, GROUP)).T[0:8, :]
+
+    for j in (3, 1, 2, 0):
+        target = members[j]
+        lax.fori_loop(0, per_member, lambda i, _: (finish(target * per_member + i), 0)[1], 0, unroll=2)
+        pieces = partial.at[pl.ds(target * per_member, per_member)]
+        if j:
+            chunk = normed.at[pl.ds(pl.multiple_of(target * own_rows, own_rows), own_rows)]
+            send(chunk, normed_in.at[member], normed_sem.at[j], (base + target, core))
+            send(pieces, partial_in.at[0, j], partial_sem.at[0, j], (base + target, core))
+        send(pieces, partial_in.at[1, j], partial_sem.at[1, j], (base + target, 1 - core))
+    normed_in[member] = normed[pl.ds(pl.multiple_of(member * own_rows, own_rows), own_rows), :]
+    penalty = partial[pl.ds(member * per_member, per_member)]
+    for j in range(PLANE):
+        if j:
+            arrived(normed_in.at[members[j]], normed_sem.at[j])
+            arrived(partial_in.at[0, j], partial_sem.at[0, j])
+            penalty = penalty + partial_in[0, j]
+        arrived(partial_in.at[1, j], partial_sem.at[1, j])
+        penalty = penalty + partial_in[1, j]
+    penalty = penalty * (1.0 / (channels * PLANE * lax.axis_size("tp")) ** 0.5)
+    for i in range(per_member):
+        turned = jnp.broadcast_to(penalty[i][0:1, :], (GROUP, GROUP)).T
+        turned = jnp.concatenate([turned] * (channels // GROUP), 1)
+        span = pl.ds(i * GROUP, GROUP)
+        for j in range(PLANE):
+            value = normed_in[j, span, :].astype(F32) - turned * steer[:, j * channels : (j + 1) * channels]
+            out_ref[j, span, :] = value.astype(BF16)
+    for copy, when in started:
+        if when is None:
+            copy.wait_send()
+        else:
+            pl.when(when)(lambda copy=copy: copy.wait_send())
+
+
+def per_device(tokens, x_weight, bc_weight, dt_weight, conv_x, conv_bc, dt_bias, decay_rate, d_skip, norm_gain, initial_state, steer):
+    planes = lax.axis_size("seq") // PLANE
+    own_rows, columns = tokens.shape
+    depth, all_channels = x_weight.shape
+    all_heads = dt_weight.shape[1]
+    channels, heads = all_channels // PLANE, all_heads // PLANE
+    rows = own_rows * PLANE
+    blocks = rows // GROUP
+    quarter = bc_weight.shape[1] // PLANE
+
+    steps_w = jnp.pad(dt_weight.T.reshape(PLANE, heads, depth), ((0, 0), (0, TAIL - heads), (0, 0)))
+    pack = jnp.concatenate([bc_weight.T.reshape(PLANE, quarter, depth), steps_w], 1)
+    small = jnp.pad(jnp.stack([dt_bias, decay_rate, d_skip]), ((0, 5), (0, 128 - all_heads)))
+
+    vmem = pl.BlockSpec(memory_space=pltpu.VMEM)
+    anywhere = pl.BlockSpec(memory_space=pl.ANY)
+    dma = pltpu.SemaphoreType.DMA
+    out = pl.pallas_call(
+        functools.partial(layer_kernel, planes, heads),
+        out_shape=jax.ShapeDtypeStruct((PLANE, own_rows, channels), BF16),
+        in_specs=[anywhere] * 3 + [vmem] * 6,
+        out_specs=vmem,
+        scratch_shapes=[
+            pltpu.VMEM((2, rows, columns), BF16),
+            pltpu.VMEM((planes, PLANE, depth + quarter + TAIL, channels), BF16),
+            pltpu.VMEM((rows, channels), F32),
+            pltpu.VMEM((rows, 128), F32),
+            pltpu.VMEM((TAIL, channels), BF16),
+            pltpu.VMEM((TAIL, channels), BF16),
+            pltpu.VMEM((quarter, rows), BF16),
+            pltpu.VMEM((2 * PLANE, quarter, rows), BF16),
+            pltpu.VMEM((2 * PLANE, quarter, GROUP), BF16),
+            pltpu.VMEM((rows + TAIL, channels), F32),
+            pltpu.VMEM((rows + TAIL, 2 * N), F32),
+            pltpu.VMEM((rows, channels), BF16),
+            pltpu.VMEM((rows, 2 * N), BF16),
+            pltpu.VMEM((rows, 128), F32),
+            pltpu.VMEM((rows, 128), F32),
+            pltpu.VMEM((blocks, N, channels), F32),
+            pltpu.VMEM((blocks, 8, channels), F32),
+            pltpu.VMEM((rows, channels), F32),
+            pltpu.VMEM((N, channels), BF16),
+            pltpu.VMEM((8, channels), F32),
+            pltpu.VMEM((planes, N, channels), BF16),
+            pltpu.VMEM((planes, 8, channels), F32),
+            pltpu.VMEM((rows, channels), BF16),
+            pltpu.VMEM((blocks, 8, GROUP), F32),
+            pltpu.VMEM((PLANE, own_rows, channels), BF16),
+            pltpu.VMEM((2, PLANE, blocks // PLANE, 8, GROUP), F32),
+            dma((64 + 10 * planes,)),
+            dma((6,)),
+            dma((PLANE, 2)),
+            dma((PLANE,)),
+            dma((2, planes, PLANE)),
+            dma((3,)),
+            dma(()),
+            dma((2 * PLANE,)),
+            dma((2 * PLANE,)),
+            dma((planes,)),
+            dma((planes,)),
+            dma((PLANE,)),
+            dma((2, PLANE)),
+        ],
+        compiler_params=pltpu.CompilerParams(collective_id=0, has_side_effects=True, vmem_limit_bytes=48 * 2**20),
+    )(
+        tokens, x_weight, pack, conv_x, conv_bc, small, norm_gain[None, :],
+        initial_state.reshape(all_channels, N), steer[None, :],
+    )
+    return out.transpose(1, 0, 2).reshape(own_rows, all_channels)
+
+
 def solution(mesh):
     placed = (
         P("seq", "tp"),
@@ -169,6 +644,7 @@
         P("tp", None, None),
         P("tp"),
     )
+    planar = mesh.shape["tp"] == 2 and mesh.shape["seq"] % PLANE == 0
     return jax.shard_map(
-        per_device, mesh=mesh, in_specs=placed, out_specs=P("seq", "tp"), check_vma=False
-    )
+        per_device if planar else portable, mesh=mesh, in_specs=placed, out_specs=P("seq", "tp"), check_vma=False
+    )

time: 347 us -> 89.5 us (0.26)
  waiting for transfers between devices: 173 us -> 0 us
  blocking collectives: 83.6 us -> 0 us
  Pallas kernels: 0 us -> 82.2 us
  local copies, waits for them, and re-layouts: 33.8 us -> 6.85 us
  other arithmetic: 22.2 us -> 0.02 us
  matrix products: 15.1 us -> 0 us
  between operations: 13.3 us -> 0.08 us
  starting transfers between devices: 3.75 us -> 0 us
    all_gather x4 -> x0, waiting for transfers between devices: 171 us -> none  [the longest x1 111 us: per_device(): lax.all_gather(x_weight, 'seq', axis=0, tiled=True)]
    pallas_call x0 -> x1, Pallas kernels: none -> 82.2 us  [per_device(): pl.pallas_call(functools.partial(layer_kernel, planes, heads), out_shape=...]
    all_gather x3 -> x0, blocking collectives: 81.1 us -> none  [the longest x1 39.7 us: per_device(): lax.all_gather(dt_weight, 'seq', axis=0, tiled=True)]
    dynamic_update_slice x2 -> x0, local copies, waits for them, and re-layouts: 26.1 us -> none  [per_device(): local_state, local_out = lax.scan(block_update, zero_state, inputs)]
    select_n x32 -> x0, other arithmetic: 17.9 us -> none  [turn(): return jax.tree.map(lambda a, b: jnp.where(reached, a, b), new, before)]
    dot_general x12 -> x0, matrix products: 15.1 us -> none  [the longest x1 6.43 us: per_device(): jnp.dot(source, lax.all_gather(x_weight, 'seq', axis=0, tiled=True), pref...]
    ppermute x1 -> x0, starting transfers between devices: 3.63 us -> none  [passed_along(): lax.ppermute(value, axis, [(source, source + steps) for source in range(f...]
    unnamed x12 -> x22, local copies, waits for them, and re-layouts: 1.09 us -> 4.7 us
  transfers between devices with their start and end apart: 5 -> 0, of which waited for: 4 -> 0; matrix products, arithmetic and copies ran while one was open for 3% -> 0% of each run, Pallas kernels for 0% -> 0%
where the time goes in v2:
time: 89.5 us; the launch traced here: 89.1 us
  Pallas kernels  82.2 us (92%)
  local copies, waits for them, and re-layouts  6.85 us (8%)
    pallas_call x1, Pallas kernels, per_device(): pl.pallas_call(functools.partial(layer_kernel, planes, heads), out_shape=...  82.2 us
    unnamed x22, local copies, waits for them, and re-layouts  4.7 us

profile of v2, /device:TPU:0, one launch (start us, length us, event | category | flops | bytes accessed | tf_op | source)
XLA Modules:
  0.0 89.1 jit_solution(7641732614553725085)
XLA Ops:
  0.0 0.0 copy-start.7
  0.0 0.0 copy-start.8
  0.0 0.0 copy-start.9
  0.0 0.0 copy-start.10
  0.0 0.7 copy-done.8
  0.7 0.0 copy-done.9
  0.7 0.0 copy-done.10
  0.7 0.0 copy-done.7
  0.7 0.9 %copy.14 = bf16[128,256]{1,0:T(8,128)(2,1)S(1)} copy(bf16[128,256]{0,1:T(8,128)(2,1)} %bitcast.17) | data formatting | bytes 131072 | tf_op jit(solution)/shard_map/transpose | solution.py:572
  1.7 0.0 copy-start.3
  1.7 0.0 copy-start.4
  1.7 0.0 copy-start.5
  1.7 0.0 copy-start.6
  1.8 0.7 copy-done.3
  2.4 0.0 copy-done.4
  2.4 0.0 copy-done.5
  2.4 0.0 copy-done.6
  2.4 0.0 copy-start
  2.4 1.2 %copy-done = bf16[256,2048]{1,0:T(8,128)(2,1)S(1)} copy-done((bf16[256,2048]{1,0:T(8,128)(2,1)S(1)}, bf16[256,2048]{1,0:T(8,128)(2,1)}, u32[]{:S(2)}) %copy-start) | copy-done | bytes 1048600
  3.7 0.0 copy-start.1
  3.7 1.0 %copy-done.1 = bf16[256,1024]{1,0:T(8,128)(2,1)S(1)} copy-done((bf16[256,1024]{1,0:T(8,128)(2,1)S(1)}, bf16[256,1024]{1,0:T(8,128)(2,1)}, u32[]{:S(2)}) %copy-start.1) | copy-done | bytes 524312
  4.7 0.0 copy-start.2
  4.7 1.0 %copy-done.2 = f32[16,64,128]{2,1,0:T(8,128)S(1)} copy-done((f32[16,64,128]{2,1,0:T(8,128)S(1)}, f32[16,64,128]{2,1,0:T(8,128)}, u32[]{:S(2)}) %copy-start.2) | copy-done | bytes 524312
  5.7 82.2 %shard_map.118 = bf16[4,256,256]{2,1,0:T(8,128)(2,1)S(1)} custom-call(bf16[256,2048]{1,0:T(8,128)(2,1)S(1)} %copy-done, bf16[256,1024]{1,0:T(8,128)(2,1)S(1)} %copy-done.1, bf16[4,48,256]{2,1,0:T(8,128)(2,1)S(1)} %fusion.1.pack_ref, f32[4,1024]{1,0:T(4,128)S(1)} %copy-done.3, f32[4,256]{1,0:T(4,128)S(1)} %copy-done.4, ...), custom_call_target="tpu_custom_call" | custom-call | tf_op jit(solution)/shard_map/pallas_call | solution.py:578
  87.9 0.2 copy.15
  88.1 1.0 %copy.16 = bf16[256,1024]{1,0:T(8,128)(2,1)} copy(bf16[256,1024]{0,1:T(8,128)(2,1)S(1)} %bitcast.15) | data formatting | bytes 1048576 | tf_op jit(solution)/shard_map/reshape | solution.py:629
  (3 shorter events, 0.0 us)
Async XLA Ops:
  0.0 0.7 copy-start.7
  0.0 0.7 copy-start.8
  0.0 0.7 copy-start.9
  0.0 0.7 copy-start.10
  1.7 0.7 copy-start.3
  1.7 0.7 copy-start.4
  1.7 0.7 copy-start.5
  1.7 0.7 copy-start.6
  2.4 1.2 %copy-start = (bf16[256,2048]{1,0:T(8,128)(2,1)S(1)}, bf16[256,2048]{1,0:T(8,128)(2,1)}, u32[]{:S(2)}) copy-start(bf16[256,2048]{1,0:T(8,128)(2,1)} %tok_ref.1) | copy-start | bytes 3145732
  3.7 1.0 %copy-start.1 = (bf16[256,1024]{1,0:T(8,128)(2,1)S(1)}, bf16[256,1024]{1,0:T(8,128)(2,1)}, u32[]{:S(2)}) copy-start(bf16[256,1024]{1,0:T(8,128)(2,1)} %xw_ref.1) | copy-start | bytes 1572868
  4.7 1.0 %copy-start.2 = (f32[16,64,128]{2,1,0:T(8,128)S(1)}, f32[16,64,128]{2,1,0:T(8,128)}, u32[]{:S(2)}) copy-start(f32[16,64,128]{2,1,0:T(8,128)} %param.22) | copy-start | bytes 1572868

commit v3 on v2

--- a/solution.py
+++ b/solution.py
@@ -192,7 +192,8 @@
 
 
 def layer_kernel(
-    planes, heads, tok_ref, xw_ref, pack_ref, taps_x, taps_bc, small, gain, first, steer, out_ref,
+    planes, heads, tok_ref, xw_ref, bcw_hbm, dtw_hbm, taps_x_hbm, taps_bc_hbm, bias_hbm, rate_hbm, skip_hbm, gain_hbm, first_hbm, steer_hbm, out_ref,
+    bcw, dtw, pack_ref, taps_x, taps_bc, small_in, small, gain, first, steer, load_sem,
     toks, weights, wide, narrow, x_tail, x_last, bc_own, bc_all, bc_tail,
     x_pad, bc_pad, x_conv, bc_conv, s_keep, dt_keep, states, logs, y_keep, state_out, total_out, state_in, total_in,
     normed, partial, normed_in, partial_in,
@@ -219,6 +220,14 @@
     far = [lax.rem(plane + j, planes) for j in range(planes)]
     has_below, has_above = plane > 0, plane < planes - 1
 
+    loads = [
+        (bcw_hbm, bcw), (dtw_hbm, dtw), (taps_x_hbm, taps_x), (taps_bc_hbm, taps_bc), (bias_hbm, small_in.at[0]),
+        (rate_hbm, small_in.at[1]), (skip_hbm, small_in.at[2]), (gain_hbm, gain), (steer_hbm, steer),
+        (first_hbm.at[pl.ds(pl.multiple_of(member * channels, channels), channels)], first),
+    ]
+    loads = [pltpu.make_async_copy(source, target, load_sem.at[i]) for i, (source, target) in enumerate(loads)]
+    for copy in loads:
+        copy.start()
     barrier = pltpu.get_barrier_semaphore()
 
     def greet(s, c):
@@ -286,21 +295,35 @@
     def quarter_of(m):
         return xw_ref.at[:, pl.ds(pl.multiple_of(m * channels, channels), channels)]
 
-    def both(m, slot, sem, device, when=None):
-        send(quarter_of(m), weights.at[plane, slot, pl.ds(0, depth)], sem, device, when)
-        send(pack_ref.at[m], weights.at[plane, slot, pl.ds(depth, quarter + TAIL)], sem, device, when)
+    def wide_part(m, *where):
+        send(quarter_of(m), weights.at[plane, member, pl.ds(0, depth)], *where)
+
+    def thin_part(m, *where):
+        send(pack_ref.at[m], weights.at[plane, member, pl.ds(depth, quarter + TAIL)], *where)
 
     own_copies = [
         pltpu.make_async_copy(quarter_of(member), weights.at[plane, member, pl.ds(0, depth)], own_sem.at[0]),
         pltpu.make_async_copy(pack_ref.at[member], weights.at[plane, member, pl.ds(depth, quarter + TAIL)], own_sem.at[1]),
         pltpu.make_async_copy(tok_ref, toks.at[core, pl.ds(pl.multiple_of(member * own_rows, own_rows), own_rows)], own_sem.at[2]),
     ]
-    for copy in own_copies:
-        copy.start()
-    for j in (1, 2, 3):
-        both(members[j], member, swap_sem.at[j], across[j])
-    both(member, member, line_sem.at[0, 1, 0], up, has_above)
-    both(member, member, line_sem.at[1, 1, 0], down, has_below)
+    own_copies[0].start()
+    own_copies[2].start()
+
+    def first_parts(part):
+        for j in (1, 2, 3):
+            part(members[j], swap_sem.at[j], across[j])
+        part(member, line_sem.at[0, 1, 0], up, has_above)
+        part(member, line_sem.at[1, 1, 0], down, has_below)
+
+    first_parts(wide_part)
+    loads[0].wait()
+    loads[1].wait()
+    turned = bcw[...].astype(F32).T.astype(BF16)
+    for m in range(PLANE):
+        pack_ref[m, 0:quarter, :] = turned[m * quarter : (m + 1) * quarter]
+        pack_ref[m, quarter:, :] = dtw[...]
+    own_copies[1].start()
+    first_parts(thin_part)
     send(own_piece(0), piece(core, 0, 0), tok_sem.at[0], across[1])
     send(own_piece(1), piece(core, 0, 1), tok_sem.at[2], across[2])
     send(own_piece(1), piece(core, 0, 1), tok_sem.at[1], across[1])
@@ -389,10 +412,9 @@
     for i in range(PLANE):
         part = rows // PLANE
         bc_own[:, i * part : (i + 1) * part] = narrow[i * part : (i + 1) * part, :].T[0:quarter, :].astype(BF16)
-    for j in range(PLANE):
-        for c in (core, 1 - core):
-            if j or c is not core:
-                send(bc_own, bc_all.at[me], bc_sem.at[me], (base + members[j], c))
+    for j in (3, 1, 2):
+        send(bc_own, bc_all.at[me], bc_sem.at[me], across[j])
+    send(bc_own, bc_all.at[me], bc_sem.at[me], sibling)
     last = bc_own.at[:, pl.ds(rows - GROUP, GROUP)]
     for m in range(PLANE):
         for c in range(2):
@@ -400,6 +422,11 @@
     bc_all[me] = bc_own[...]
 
     mine = pl.ds(pl.multiple_of(member * channels, channels), channels)
+    for copy in loads[2:]:
+        copy.wait()
+    small[...] = jnp.zeros_like(small)
+    for i in range(3):
+        small[i : i + 1, 0 : PLANE * heads] = small_in[i]
     own_small = pltpu.roll(small[...], lax.rem(128 - member * heads, 128), 1)
     bias, rate = own_small[0:1, :], own_small[1:2, :]
     skip = spread(own_small, heads, size)[2:3, :]
@@ -414,7 +441,7 @@
         return pl.ds(pl.multiple_of(at * GROUP, GROUP), GROUP)
 
     def steps_of(at, _):
-        raw = pltpu.roll(narrow[here(at), :], 128 - quarter, 1) + bias
+        raw = pltpu.roll(narrow[here(at), :], 128 - quarter - member * heads, 1) + bias
         dt = jnp.maximum(raw, 0.0) + jnp.log1p(jnp.exp(-jnp.abs(raw)))
         a = -dt * rate
         one = a.astype(BF16)
@@ -427,6 +454,10 @@
         return 0
 
     lax.fori_loop(0, blocks, steps_of, 0, unroll=2)
+    for j in (1, 2, 3):
+        slot = core * PLANE + members[j]
+        arrived(bc_all.at[slot], bc_sem.at[slot])
+        send(bc_all.at[slot], bc_all.at[slot], bc_sem.at[slot], sibling)
 
     @pl.when(jnp.logical_not(has_below))
     def _():
@@ -443,10 +474,8 @@
     lax.fori_loop(0, blocks, convolved, 0, unroll=2)
 
     for j in range(PLANE):
-        for c in (core, 1 - core):
-            if j or c is not core:
-                sender = c * PLANE + members[j]
-                arrived(bc_all.at[sender], bc_sem.at[sender])
+        slot = (1 - core) * PLANE + members[j]
+        arrived(bc_all.at[slot], bc_sem.at[slot])
     for sender in range(2 * PLANE):
         arrived(bc_tail.at[sender], bct_sem.at[sender], has_below)
     bc_pad[0:TAIL, :] = bc_tail[...].astype(F32).reshape(2 * N, GROUP).T[GROUP - TAIL :, :]
@@ -500,7 +529,7 @@
 
     lax.fori_loop(0, blocks, inside, 0, unroll=2)
 
-    entering = first[pl.ds(pl.multiple_of(member * channels, channels), channels), :].T
+    entering = first[...].T
     for j in range(1, planes):
         arrived(state_in.at[j], state_sem.at[j])
         arrived(total_in.at[j], total_sem.at[j])
@@ -550,7 +579,7 @@
         span = pl.ds(i * GROUP, GROUP)
         for j in range(PLANE):
             value = normed_in[j, span, :].astype(F32) - turned * steer[:, j * channels : (j + 1) * channels]
-            out_ref[j, span, :] = value.astype(BF16)
+            out_ref[span, j * channels : (j + 1) * channels] = value.astype(BF16)
     for copy, when in started:
         if when is None:
             copy.wait_send()
@@ -568,19 +597,26 @@
     blocks = rows // GROUP
     quarter = bc_weight.shape[1] // PLANE
 
-    steps_w = jnp.pad(dt_weight.T.reshape(PLANE, heads, depth), ((0, 0), (0, TAIL - heads), (0, 0)))
-    pack = jnp.concatenate([bc_weight.T.reshape(PLANE, quarter, depth), steps_w], 1)
-    small = jnp.pad(jnp.stack([dt_bias, decay_rate, d_skip]), ((0, 5), (0, 128 - all_heads)))
-
     vmem = pl.BlockSpec(memory_space=pltpu.VMEM)
-    anywhere = pl.BlockSpec(memory_space=pl.ANY)
+    far = pl.BlockSpec(memory_space=pltpu.HBM)
     dma = pltpu.SemaphoreType.DMA
     out = pl.pallas_call(
         functools.partial(layer_kernel, planes, heads),
-        out_shape=jax.ShapeDtypeStruct((PLANE, own_rows, channels), BF16),
-        in_specs=[anywhere] * 3 + [vmem] * 6,
+        out_shape=jax.ShapeDtypeStruct((own_rows, all_channels), BF16),
+        in_specs=[far] * 12,
         out_specs=vmem,
         scratch_shapes=[
+            pltpu.VMEM(bc_weight.shape, BF16),
+            pltpu.VMEM((all_heads, depth), BF16),
+            pltpu.VMEM((PLANE, quarter + TAIL, depth), BF16),
+            pltpu.VMEM(conv_x.shape, F32),
+            pltpu.VMEM(conv_bc.shape, F32),
+            pltpu.VMEM((3, 1, all_heads), F32),
+            pltpu.VMEM((8, 128), F32),
+            pltpu.VMEM((1, all_channels), F32),
+            pltpu.VMEM((channels, N), F32),
+            pltpu.VMEM((1, all_channels), F32),
+            dma((10,)),
             pltpu.VMEM((2, rows, columns), BF16),
             pltpu.VMEM((planes, PLANE, depth + quarter + TAIL, channels), BF16),
             pltpu.VMEM((rows, channels), F32),
@@ -621,12 +657,12 @@
             dma((PLANE,)),
             dma((2, PLANE)),
         ],
-        compiler_params=pltpu.CompilerParams(collective_id=0, has_side_effects=True, vmem_limit_bytes=48 * 2**20),
+        compiler_params=pltpu.CompilerParams(collective_id=0, has_side_effects=True, vmem_limit_bytes=60 * 2**20),
     )(
-        tokens, x_weight, pack, conv_x, conv_bc, small, norm_gain[None, :],
-        initial_state.reshape(all_channels, N), steer[None, :],
-    )
-    return out.transpose(1, 0, 2).reshape(own_rows, all_channels)
+        tokens, x_weight, bc_weight, dt_weight.T, conv_x, conv_bc, dt_bias[None, :], decay_rate[None, :], d_skip[None, :],
+        norm_gain[None, :], initial_state.reshape(all_channels, N), steer[None, :],
+    )
+    return out
 
 
 def solution(mesh):

time: 89.5 us -> 83.6 us (0.934)
  local copies, waits for them, and re-layouts: 6.85 us -> 1.87 us
    unnamed x22 -> x1, local copies, waits for them, and re-layouts: 4.7 us -> 1.87 us
    transpose x2 -> x0, local copies, waits for them, and re-layouts: 1.14 us -> none  [the longest x1 0.94 us: per_device(): bc_weight.T.reshape(PLANE, quarter, depth)]
    reshape x2 -> x0, local copies, waits for them, and re-layouts: 1.01 us -> none  [the longest x1 1 us: per_device(): return out.transpose(1, 0, 2).reshape(own_rows, all_channels)]
where the time goes in v3:
time: 83.6 us; the launch traced here: 83.5 us
  Pallas kernels  81.6 us (98%)
  local copies, waits for them, and re-layouts  1.87 us (2%)
    pallas_call x1, Pallas kernels, per_device(): pl.pallas_call(functools.partial(layer_kernel, planes, heads), out_shape=...  81.6 us
    unnamed x1, local copies, waits for them, and re-layouts  1.87 us

profile of v3, /device:TPU:0, one launch (start us, length us, event | category | flops | bytes accessed | tf_op | source)
XLA Modules:
  0.0 83.5 jit_solution(6473632453520317593)
XLA Ops:
  0.0 81.6 %shard_map.118 = bf16[256,1024]{1,0:T(8,128)(2,1)} custom-call(bf16[256,2048]{1,0:T(8,128)(2,1)} %tok_ref.1, bf16[256,1024]{1,0:T(8,128)(2,1)} %xw_ref.1, bf16[256,128]{1,0:T(8,128)(2,1)} %bcw_hbm.1, bf16[16,256]{1,0:T(8,128)(2,1)} %bitcast.8, f32[4,1024]{1,0:T(4,128)} %taps_x_hbm.1, f32[4,256]{1,0:T(4,128)} %taps_bc_hbm.1, f32[1,16]{1,0:T(1,128)} %bitcast.11, ...), custom_call_target="tpu_custom_call" | custom-call | tf_op jit(solution)/shard_map/pallas_call | solution.py:603
  81.6 1.9 %copy.14 = bf16[256,1024]{1,0:T(8,128)(2,1)} copy(bf16[256,1024]{1,0:T(8,128)(2,1)} %shard_map.118) | data formatting | bytes 1048576

commit v4 on v3

--- a/solution.py
+++ b/solution.py
@@ -184,17 +184,18 @@
 
 
 def spread(values, heads, size):
-    lane = lax.broadcasted_iota(jnp.int32, (values.shape[0], heads * size), 1)
-    wide = jnp.broadcast_to(values[:, heads - 1 : heads], lane.shape)
-    for h in range(heads - 2, -1, -1):
-        wide = jnp.where(lane < (h + 1) * size, values[:, h : h + 1], wide)
-    return wide
+    head = lax.broadcasted_iota(jnp.int32, (128, heads * size), 0)
+    lane = lax.broadcasted_iota(jnp.int32, (128, heads * size), 1)
+    chosen = (head == lane // size).astype(BF16)
+    high = values.astype(BF16)
+    low = (values - high.astype(F32)).astype(BF16)
+    return dot(high, chosen) + dot(low, chosen)
 
 
 def layer_kernel(
     planes, heads, tok_ref, xw_ref, bcw_hbm, dtw_hbm, taps_x_hbm, taps_bc_hbm, bias_hbm, rate_hbm, skip_hbm, gain_hbm, first_hbm, steer_hbm, out_ref,
     bcw, dtw, pack_ref, taps_x, taps_bc, small_in, small, gain, first, steer, load_sem,
-    toks, weights, wide, narrow, x_tail, x_last, bc_own, bc_all, bc_tail,
+    toks, weights, thin, wide, narrow, x_tail, x_last, bc_own, bc_all, bc_tail,
     x_pad, bc_pad, x_conv, bc_conv, s_keep, dt_keep, states, logs, y_keep, state_out, total_out, state_in, total_in,
     normed, partial, normed_in, partial_in,
     send_sem, tok_sem, sib_sem, swap_sem, line_sem, own_sem, tail_sem, bct_sem, bc_sem, state_sem, total_sem, normed_sem, partial_sem,
@@ -356,7 +357,16 @@
         for h in range(2):
             arrived(piece(1 - core, j, h), sib_sem.at[j, h])
 
-    filler = jnp.zeros((128 - quarter - TAIL, depth), BF16)
+    filler = jnp.zeros((128 - quarter - TAIL, depth), F32)
+
+    def turn(lowest, highest):
+        def one(p, _):
+            for k in range(PLANE):
+                block_rows = jnp.concatenate([weights[p, k, depth:, :].astype(F32), filler], 0)
+                thin[p * PLANE + k] = block_rows.T.astype(BF16)
+            return 0
+
+        lax.fori_loop(lowest, highest, one, 0)
 
     def multiply(j, p):
         where = pl.ds(pl.multiple_of(member_at(j) * own_rows, own_rows), own_rows)
@@ -367,8 +377,7 @@
             span = pl.ds(pl.multiple_of((p % per_core) * (PLANE * depth) + k * depth, depth), depth)
             left = toks[side, where, span]
             total_wide += dot(left, weights[p, k, 0:depth, :])
-            turned = jnp.concatenate([weights[p, k, depth:, :], filler], 0)
-            total_narrow += lax.dot_general(left, turned, (((1,), (1,)), ((), ())), preferred_element_type=F32)
+            total_narrow += dot(left, thin[p * PLANE + k])
         wide[where, :] = total_wide
         narrow[where, :] = total_narrow
 
@@ -397,10 +406,14 @@
                 copy.wait()
             for i in range(3):
                 from_sibling(i)
+            turn(near_low, near_high)
             multiply_all((0, 3), near_low, near_high)
+            token(3, 0, 4)
+        if at == len(steps) - 1:
+            token(3, 1, 5)
         relay(step, j)
-    token(3, 0, 4)
-    token(3, 1, 5)
+    turn(0, near_low)
+    turn(near_high, planes)
     multiply_all((0, 3), 0, near_low)
     multiply_all((0, 3), near_high, planes)
     from_sibling(3)
@@ -453,7 +466,7 @@
         x_pad[pl.ds(pl.multiple_of(at * GROUP + TAIL, TAIL), GROUP), :] = wide[here(at), :].astype(BF16).astype(F32)
         return 0
 
-    lax.fori_loop(0, blocks, steps_of, 0, unroll=2)
+    lax.fori_loop(0, blocks, steps_of, 0, unroll=4)
     for j in (1, 2, 3):
         slot = core * PLANE + members[j]
         arrived(bc_all.at[slot], bc_sem.at[slot])
@@ -471,7 +484,7 @@
         x_conv[here(at), :] = smooth(x_pad, at, taps)
         return 0
 
-    lax.fori_loop(0, blocks, convolved, 0, unroll=2)
+    lax.fori_loop(0, blocks, convolved, 0, unroll=4)
 
     for j in range(PLANE):
         slot = (1 - core) * PLANE + members[j]
@@ -485,7 +498,7 @@
         bc_pad[pl.ds(pl.multiple_of(at * GROUP + TAIL, TAIL), GROUP), :] = turned.T
         return 0
 
-    lax.fori_loop(0, blocks, unturned, 0, unroll=2)
+    lax.fori_loop(0, blocks, unturned, 0, unroll=4)
 
     def advance(at, carry):
         state, log = carry
@@ -498,12 +511,12 @@
         weight = spread(jnp.exp(end - s) * dt_keep[here(at), :], heads, size)
         scaled = (x_conv[here(at), :].astype(F32) * weight).astype(BF16)
         b_turned = bc[:, :N].astype(F32).T.astype(BF16)
-        ended = spread(jnp.broadcast_to(end, (8, GROUP)), heads, size)
-        state = jnp.exp(ended[0:1, :]) * state + dot(b_turned, scaled)
+        ended = jnp.broadcast_to(end, (8, 128))
+        state = spread(jnp.exp(ended), heads, size)[0:1, :] * state + dot(b_turned, scaled)
         return state, log + ended
 
-    zeros = (jnp.zeros((N, channels), F32), jnp.zeros((8, channels), F32))
-    state, log = lax.fori_loop(0, blocks, advance, zeros, unroll=2)
+    zeros = (jnp.zeros((N, channels), F32), jnp.zeros((8, 128), F32))
+    state, log = lax.fori_loop(0, blocks, advance, zeros, unroll=4)
     state_out[...] = state.astype(BF16)
     total_out[...] = log
     for j in range(1, planes):
@@ -527,14 +540,14 @@
         y_keep[here(at), :] = jnp.concatenate(parts, 1) + skip * x.astype(F32)
         return 0
 
-    lax.fori_loop(0, blocks, inside, 0, unroll=2)
+    lax.fori_loop(0, blocks, inside, 0, unroll=4)
 
     entering = first[...].T
     for j in range(1, planes):
         arrived(state_in.at[j], state_sem.at[j])
         arrived(total_in.at[j], total_sem.at[j])
     for j in range(1, planes):
-        later = jnp.exp(total_in[j][0:1, :]) * entering + state_in[j].astype(F32)
+        later = spread(jnp.exp(total_in[j]), heads, size)[0:1, :] * entering + state_in[j].astype(F32)
         entering = jnp.where(far[j] < plane, later, entering)
 
     group_of = lax.broadcasted_iota(jnp.int32, (2, channels, channels), 1) // size
@@ -543,8 +556,8 @@
     def finish(at):
         s = s_keep[here(at), :]
         c = bc_conv[here(at), :][:, N:]
-        state = states[at] + jnp.exp(logs[at][0:1, :]) * entering
-        y = y_keep[here(at), :] + jnp.exp(spread(s, heads, size)) * split_dot(c, state)
+        state = states[at] + spread(jnp.exp(logs[at]), heads, size)[0:1, :] * entering
+        y = y_keep[here(at), :] + spread(jnp.exp(s), heads, size) * split_dot(c, state)
         square = y * y
         high = square.astype(BF16)
         low = (square - high.astype(F32)).astype(BF16)
@@ -619,6 +632,7 @@
             dma((10,)),
             pltpu.VMEM((2, rows, columns), BF16),
             pltpu.VMEM((planes, PLANE, depth + quarter + TAIL, channels), BF16),
+            pltpu.VMEM((planes * PLANE, depth, 128), BF16),
             pltpu.VMEM((rows, channels), F32),
             pltpu.VMEM((rows, 128), F32),
             pltpu.VMEM((TAIL, channels), BF16),
@@ -633,12 +647,12 @@
             pltpu.VMEM((rows, 128), F32),
             pltpu.VMEM((rows, 128), F32),
             pltpu.VMEM((blocks, N, channels), F32),
-            pltpu.VMEM((blocks, 8, channels), F32),
+            pltpu.VMEM((blocks, 8, 128), F32),
             pltpu.VMEM((rows, channels), F32),
             pltpu.VMEM((N, channels), BF16),
-            pltpu.VMEM((8, channels), F32),
+            pltpu.VMEM((8, 128), F32),
             pltpu.VMEM((planes, N, channels), BF16),
-            pltpu.VMEM((planes, 8, channels), F32),
+            pltpu.VMEM((planes, 8, 128), F32),
             pltpu.VMEM((rows, channels), BF16),
             pltpu.VMEM((blocks, 8, GROUP), F32),
             pltpu.VMEM((PLANE, own_rows, channels), BF16),

time: 83.6 us -> 82.2 us (0.983)
  Pallas kernels: 81.6 us -> 80 us
    pallas_call x1, Pallas kernels: 81.6 us -> 80 us  [per_device(): pl.pallas_call(functools.partial(layer_kernel, planes, heads), out_shape=...]
where the time goes in v4:
time: 82.2 us; the launch traced here: 81.9 us
  Pallas kernels  80 us (97%)
  local copies, waits for them, and re-layouts  1.87 us (2%)
    pallas_call x1, Pallas kernels, per_device(): pl.pallas_call(functools.partial(layer_kernel, planes, heads), out_shape=...  80 us
    unnamed x1, local copies, waits for them, and re-layouts  1.87 us

profile of v4, /device:TPU:0, one launch (start us, length us, event | category | flops | bytes accessed | tf_op | source)
XLA Modules:
  0.0 81.9 jit_solution(10986225270337629123)
XLA Ops:
  0.0 80.0 %shard_map.118 = bf16[256,1024]{1,0:T(8,128)(2,1)} custom-call(bf16[256,2048]{1,0:T(8,128)(2,1)} %tok_ref.1, bf16[256,1024]{1,0:T(8,128)(2,1)} %xw_ref.1, bf16[256,128]{1,0:T(8,128)(2,1)} %bcw_hbm.1, bf16[16,256]{1,0:T(8,128)(2,1)} %bitcast.8, f32[4,1024]{1,0:T(4,128)} %taps_x_hbm.1, f32[4,256]{1,0:T(4,128)} %taps_bc_hbm.1, f32[1,16]{1,0:T(1,128)} %bitcast.11, ...), custom_call_target="tpu_custom_call" | custom-call | tf_op jit(solution)/shard_map/pallas_call | solution.py:616
  80.0 1.9 %copy.14 = bf16[256,1024]{1,0:T(8,128)(2,1)} copy(bf16[256,1024]{1,0:T(8,128)(2,1)} %shard_map.118) | data formatting | bytes 1048576

commit v5 on v4

--- a/solution.py
+++ b/solution.py
@@ -256,6 +256,12 @@
         distant = jnp.abs(far[j] - plane) > 1
         pl.when(distant)(lambda j=j: greet(far[j] * PLANE + member, core))
         greeted = greeted + jnp.where(distant, 1, 0)
+    loads[0].wait()
+    loads[1].wait()
+    turned = bcw[...].astype(F32).T.astype(BF16)
+    for m in range(PLANE):
+        pack_ref[m, 0:quarter, :] = turned[m * quarter : (m + 1) * quarter]
+        pack_ref[m, quarter:, :] = dtw[...]
     pl.semaphore_wait(barrier, greeted)
 
     started = []
@@ -317,12 +323,6 @@
         part(member, line_sem.at[1, 1, 0], down, has_below)
 
     first_parts(wide_part)
-    loads[0].wait()
-    loads[1].wait()
-    turned = bcw[...].astype(F32).T.astype(BF16)
-    for m in range(PLANE):
-        pack_ref[m, 0:quarter, :] = turned[m * quarter : (m + 1) * quarter]
-        pack_ref[m, quarter:, :] = dtw[...]
     own_copies[1].start()
     first_parts(thin_part)
     send(own_piece(0), piece(core, 0, 0), tok_sem.at[0], across[1])
@@ -368,59 +368,67 @@
 
         lax.fori_loop(lowest, highest, one, 0)
 
-    def multiply(j, p):
+    def multiply(j, p, total, factor):
         where = pl.ds(pl.multiple_of(member_at(j) * own_rows, own_rows), own_rows)
         per_core = columns // (PLANE * depth)
         side = p // per_core
-        total_wide, total_narrow = wide[where, :], narrow[where, :]
+        sums = total[where, :]
         for k in range(PLANE):
             span = pl.ds(pl.multiple_of((p % per_core) * (PLANE * depth) + k * depth, depth), depth)
-            left = toks[side, where, span]
-            total_wide += dot(left, weights[p, k, 0:depth, :])
-            total_narrow += dot(left, thin[p * PLANE + k])
-        wide[where, :] = total_wide
-        narrow[where, :] = total_narrow
-
-    def multiply_all(parts, lowest, highest):
+            sums += dot(toks[side, where, span], factor(p, k))
+        total[where, :] = sums
+
+    def wide_product(j, p):
+        multiply(j, p, wide, lambda p, k: weights[p, k, 0:depth, :])
+
+    def thin_product(j, p):
+        multiply(j, p, narrow, lambda p, k: thin[p * PLANE + k])
+
+    def multiply_all(parts, lowest, highest, *products):
         first_part, last_part = parts
 
+        def one(j, p):
+            for product in products:
+                product(j, p)
+
         def at(j, _):
-            return lax.fori_loop(lowest, highest, lambda p, _: (multiply(j, p), 0)[1], 0)
+            return lax.fori_loop(lowest, highest, lambda p, _: (one(j, p), 0)[1], 0)
 
         lax.fori_loop(first_part, last_part, at, 0)
+
+    def rest(product):
+        multiply_all((0, 3), 0, near_low, product)
+        multiply_all((0, 3), near_high, planes, product)
 
     wide[...] = jnp.zeros_like(wide)
     narrow[...] = jnp.zeros_like(narrow)
     takes = [
         (1, 0, 0, (4, 2)), (2, 1, 2, (5, 1)), (1, 1, 1, None), (2, 0, 3, None),
     ]
-    places = [3, 3, 6, 6]
+    places = [4, 4, 7, 7]
     near_low, near_high = jnp.maximum(plane - (planes - 2), 0), jnp.minimum(plane + planes - 1, planes)
     steps = [(step, j) for step in range(1, planes) for j in range(PLANE)]
     for at, (step, j) in enumerate(steps):
         for take, place in zip(takes, places):
             if min(place, len(steps) - 1) == at:
                 token(*take)
-        if at == len(steps) - PLANE + 1:
+        if at == len(steps) - PLANE:
             for copy in own_copies:
                 copy.wait()
             for i in range(3):
                 from_sibling(i)
             turn(near_low, near_high)
-            multiply_all((0, 3), near_low, near_high)
+            multiply_all((0, 3), near_low, near_high, wide_product, thin_product)
             token(3, 0, 4)
         if at == len(steps) - 1:
             token(3, 1, 5)
         relay(step, j)
     turn(0, near_low)
     turn(near_high, planes)
-    multiply_all((0, 3), 0, near_low)
-    multiply_all((0, 3), near_high, planes)
+    rest(thin_product)
     from_sibling(3)
-    multiply_all((3, 4), 0, planes)
-
-    x_last[...] = wide[rows - TAIL : rows, :].astype(BF16)
-    send(x_last, x_tail, tail_sem, up, has_above)
+    multiply_all((3, 4), 0, planes, thin_product)
+
     me = core * PLANE + member
     for i in range(PLANE):
         part = rows // PLANE
@@ -433,6 +441,10 @@
         for c in range(2):
             send(last, bc_tail.at[me], bct_sem.at[me], (base + PLANE + m, c), has_above)
     bc_all[me] = bc_own[...]
+    rest(wide_product)
+    multiply_all((3, 4), 0, planes, wide_product)
+    x_last[...] = wide[rows - TAIL : rows, :].astype(BF16)
+    send(x_last, x_tail, tail_sem, up, has_above)
 
     mine = pl.ds(pl.multiple_of(member * channels, channels), channels)
     for copy in loads[2:]:

time: 82.2 us -> 81.6 us (level)
  Pallas kernels: 80 us -> 79 us
    pallas_call x1, Pallas kernels: 80 us -> 79 us  [per_device(): pl.pallas_call(functools.partial(layer_kernel, planes, heads), out_shape=...]
where the time goes in v5:
time: 81.6 us; the launch traced here: 80.9 us
  Pallas kernels  79 us (97%)
  local copies, waits for them, and re-layouts  1.87 us (2%)
    pallas_call x1, Pallas kernels, per_device(): pl.pallas_call(functools.partial(layer_kernel, planes, heads), out_shape=...  79 us
    unnamed x1, local copies, waits for them, and re-layouts  1.87 us

profile of v5, /device:TPU:0, one launch (start us, length us, event | category | flops | bytes accessed | tf_op | source)
XLA Modules:
  0.0 80.9 jit_solution(392990262982125790)
XLA Ops:
  0.0 79.0 %shard_map.118 = bf16[256,1024]{1,0:T(8,128)(2,1)} custom-call(bf16[256,2048]{1,0:T(8,128)(2,1)} %tok_ref.1, bf16[256,1024]{1,0:T(8,128)(2,1)} %xw_ref.1, bf16[256,128]{1,0:T(8,128)(2,1)} %bcw_hbm.1, bf16[16,256]{1,0:T(8,128)(2,1)} %bitcast.8, f32[4,1024]{1,0:T(4,128)} %taps_x_hbm.1, f32[4,256]{1,0:T(4,128)} %taps_bc_hbm.1, f32[1,16]{1,0:T(1,128)} %bitcast.11, ...), custom_call_target="tpu_custom_call" | custom-call | tf_op jit(solution)/shard_map/pallas_call | solution.py:628
  79.1 1.9 %copy.14 = bf16[256,1024]{1,0:T(8,128)(2,1)} copy(bf16[256,1024]{1,0:T(8,128)(2,1)} %shard_map.118) | data formatting | bytes 1048576

commit v6 on v5

--- a/solution.py
+++ b/solution.py
@@ -478,7 +478,7 @@
         x_pad[pl.ds(pl.multiple_of(at * GROUP + TAIL, TAIL), GROUP), :] = wide[here(at), :].astype(BF16).astype(F32)
         return 0
 
-    lax.fori_loop(0, blocks, steps_of, 0, unroll=4)
+    lax.fori_loop(0, blocks, steps_of, 0, unroll=8)
     for j in (1, 2, 3):
         slot = core * PLANE + members[j]
         arrived(bc_all.at[slot], bc_sem.at[slot])
@@ -496,7 +496,7 @@
         x_conv[here(at), :] = smooth(x_pad, at, taps)
         return 0
 
-    lax.fori_loop(0, blocks, convolved, 0, unroll=4)
+    lax.fori_loop(0, blocks, convolved, 0, unroll=8)
 
     for j in range(PLANE):
         slot = (1 - core) * PLANE + members[j]
@@ -510,7 +510,7 @@
         bc_pad[pl.ds(pl.multiple_of(at * GROUP + TAIL, TAIL), GROUP), :] = turned.T
         return 0
 
-    lax.fori_loop(0, blocks, unturned, 0, unroll=4)
+    lax.fori_loop(0, blocks, unturned, 0, unroll=8)
 
     def advance(at, carry):
         state, log = carry
@@ -528,7 +528,7 @@
         return state, log + ended
 
     zeros = (jnp.zeros((N, channels), F32), jnp.zeros((8, 128), F32))
-    state, log = lax.fori_loop(0, blocks, advance, zeros, unroll=4)
+    state, log = lax.fori_loop(0, blocks, advance, zeros, unroll=8)
     state_out[...] = state.astype(BF16)
     total_out[...] = log
     for j in range(1, planes):
@@ -552,7 +552,7 @@
         y_keep[here(at), :] = jnp.concatenate(parts, 1) + skip * x.astype(F32)
         return 0
 
-    lax.fori_loop(0, blocks, inside, 0, unroll=4)
+    lax.fori_loop(0, blocks, inside, 0, unroll=8)
 
     entering = first[...].T
     for j in range(1, planes):

time: 81.6 us -> 81.3 us (level)
  no operation moved by 1% of the time
where the time goes in v6:
time: 81.3 us; the launch traced here: 80.6 us
  Pallas kernels  78.7 us (97%)
  local copies, waits for them, and re-layouts  1.87 us (2%)
    pallas_call x1, Pallas kernels, per_device(): pl.pallas_call(functools.partial(layer_kernel, planes, heads), out_shape=...  78.7 us
    unnamed x1, local copies, waits for them, and re-layouts  1.87 us

profile of v6, /device:TPU:0, one launch (start us, length us, event | category | flops | bytes accessed | tf_op | source)
XLA Modules:
  0.0 80.6 jit_solution(10815519736381427530)
XLA Ops:
  0.0 78.7 %shard_map.118 = bf16[256,1024]{1,0:T(8,128)(2,1)} custom-call(bf16[256,2048]{1,0:T(8,128)(2,1)} %tok_ref.1, bf16[256,1024]{1,0:T(8,128)(2,1)} %xw_ref.1, bf16[256,128]{1,0:T(8,128)(2,1)} %bcw_hbm.1, bf16[16,256]{1,0:T(8,128)(2,1)} %bitcast.8, f32[4,1024]{1,0:T(4,128)} %taps_x_hbm.1, f32[4,256]{1,0:T(4,128)} %taps_bc_hbm.1, f32[1,16]{1,0:T(1,128)} %bitcast.11, ...), custom_call_target="tpu_custom_call" | custom-call | tf_op jit(solution)/shard_map/pallas_call | solution.py:628
  78.7 1.9 %copy.14 = bf16[256,1024]{1,0:T(8,128)(2,1)} copy(bf16[256,1024]{1,0:T(8,128)(2,1)} %shard_map.118) | data formatting | bytes 1048576
